TPU v7x, 32 devices: a whole 2x2x4 slice. The times are simulated.
32 devices in a mesh: dp: 8 (over z, x), feat: 4 (over y, core).
Axes of the slice: x: 2, y: 2, z: 4, core: 2. Of those that a mesh axis runs over, the one named last changes fastest.
Arguments:
- residual: bfloat16 [192, 7168], P('dp'), may hold values from -6 to 6
- cotangent: bfloat16 [192, 7168], P('dp'), may hold values from -6 to 6
- encoder_weight: bfloat16 [7168, 65536], P('dp', 'feat'), may hold values from -0.0625 to 0.0625
- encoder_bias: float32 [65536], P('feat'), may hold values from -3 to 3
- decoder_weight: bfloat16 [65536, 7168], P('feat', 'dp'), may hold values from -0.0625 to 0.0625
- route_experts: int32 [192, 8], P('dp'), may hold values from 0 to 255, all different within a row
- route_buckets: int32 [192, 8], P('dp'), may hold values from 1 to 8
Outputs:
- expert_credit: float32 [256, 65536], P('dp', 'feat')
Inputs may be any that keep to these rules, and one draw needn't show every extreme that they name: `route_experts`: each token names 8 different experts, and every expert is named by some token.
All inputs are finite; a program needn't handle non-finite values.
Results may differ from a plain program's by a relative error of at most 0.0003.
Values may be sent and summed in bfloat16 or wider, within the bound.
No kernel may reach another device: no remote copies, remote signals or barrier semaphores. Data moves between devices by JAX's collectives and lax.ppermute only.
A program may use at most 128 MiB of HBM per device.

v0:
```python
import jax
import jax.numpy as jnp
from jax import lax
from jax.sharding import PartitionSpec as P

E = 256


def routing_table(experts, buckets):
    expert_ids = jnp.arange(E, dtype=jnp.int32)
    weights = buckets.astype(jnp.float32) * 0.125
    return jnp.sum(
        (experts[:, :, None] == expert_ids[None, None, :]).astype(jnp.float32)
        * weights[:, :, None],
        axis=1,
    )


def reduce_partials(encoder_term, decoder_term, share):
    pre = lax.psum_scatter(
        encoder_term(jnp.int32(0), share * lax.axis_size("dp")),
        "dp",
        scatter_dimension=0,
        tiled=True,
    )
    grad = lax.psum_scatter(
        decoder_term(jnp.int32(0), share * lax.axis_size("dp")),
        "dp",
        scatter_dimension=0,
        tiled=True,
    )
    return (pre, grad)


def on_device(
    residual, cotangent, encoder_weight, encoder_bias, decoder_weight, route_experts, route_buckets
):
    gathered, tangent_rows = (
        lax.all_to_all(residual, "dp", split_axis=1, concat_axis=0, tiled=True),
        lax.all_to_all(cotangent, "dp", split_axis=1, concat_axis=0, tiled=True),
    )

    def encoder_term(first, count):
        return jnp.dot(gathered, encoder_weight, preferred_element_type=jnp.float32)

    def decoder_term(first, count):
        return lax.dot_general(
            tangent_rows,
            decoder_weight,
            (((1,), (1,)), ((), ())),
            preferred_element_type=jnp.float32,
        )

    pre_rows, grad_rows = reduce_partials(encoder_term, decoder_term, residual.shape[0])
    score = jnp.maximum(pre_rows + encoder_bias[None, :], 0.0) * grad_rows
    routing = routing_table(route_experts, route_buckets)
    credit_part = lax.dot_general(
        routing, score, (((0,), (0,)), ((), ())), precision=lax.Precision.HIGHEST
    )
    return lax.psum_scatter(credit_part, "dp", scatter_dimension=0, tiled=True)


def solution(mesh):
    placed = (
        P("dp", None),
        P("dp", None),
        P("dp", "feat"),
        P("feat"),
        P("feat", "dp"),
        P("dp", None),
        P("dp", None),
    )
    return jax.shard_map(
        on_device, mesh=mesh, in_specs=placed, out_specs=P("dp", "feat"), check_vma=False
    )
```

profile of v0, /device:TPU:0, one launch (start us, length us, event | category | flops | bytes accessed | tf_op | source)
XLA Modules:
  0.0 772.5 jit_solution(7524311778869174651)
XLA Ops:
  6.5 0.0 reduce-scatter.6.cloned.1.call-start
  6.5 1.0 copy.28
  7.5 18.2 %all_to_all.38 = bf16[24,8,896]{2,0,1:T(8,128)(2,1)S(1)} all-to-all(bf16[24,8,896]{2,0,1:T(8,128)(2,1)S(1)} %bitcast.20), channel_id=1, replica_groups=mesh['dp'=8,'feat'=4] {'dp'}, dimensions={1} | all-to-all | bytes 688128 | tf_op jit(solution)/shard_map/all_to_all | solution.py:40
  25.8 18.8 %fusion.8 = f32[192,16384]{1,0:T(8,128)} fusion(bf16[192,896]{1,0:T(8,128)(2,1)S(1)} %bitcast.24, bf16[16384,896]{1,0:T(8,128)(2,1)} %param.11), kind=kOutput, calls=%fused_computation.13 | convolution fusion | flops 5637144576 | bytes 42287104 | tf_op jit(solution)/shard_map/dot_general | solution.py:47
  44.6 0.0 copy-start
  44.6 0.0 reduce-scatter.6.cloned.1.call-update
  44.6 0.0 reduce-scatter.4.cloned.1.call-start
  44.7 0.9 copy-done
  45.6 23.5 %all_to_all.39 = bf16[24,8,896]{2,0,1:T(8,128)(2,1)S(1)} all-to-all(bf16[24,8,896]{2,0,1:T(8,128)(2,1)S(1)} %bitcast.21), channel_id=1, replica_groups=mesh['dp'=8,'feat'=4] {'dp'}, dimensions={1} | all-to-all | bytes 688128 | tf_op jit(solution)/shard_map/all_to_all | solution.py:39
  69.1 15.7 %fusion.7 = f32[192,16384]{1,0:T(8,128)} fusion(bf16[192,896]{1,0:T(8,128)(2,1)S(1)} %bitcast.19, bf16[896,16384]{1,0:T(8,128)(2,1)} %param.9), kind=kOutput, calls=%fused_computation.12 | convolution fusion | flops 5637144576 | bytes 42287104 | tf_op jit(solution)/shard_map/dot_general | solution.py:44
  84.8 0.0 copy-start.2
  84.8 0.0 reduce-scatter.4.cloned.1.call-update
  84.9 0.0 reduce-scatter.8.cloned.1.call-start
  84.9 0.6 copy-done.2
  85.5 0.1 copy.21
  85.6 0.0 copy-done.3
  85.6 0.1 copy.20
  85.7 0.1 select_reduce_fusion
  85.8 171.9 %reduce-scatter.6.cloned.1.call-done = f32[24,16384]{1,0:T(8,128)} async-done(((f32[192,16384]{1,0:T(8,128)}), f32[24,16384]{1,0:T(8,128)}) %reduce-scatter.6.cloned.1.call-update) | async-done | bytes 1572880 | tf_op jit(solution)/shard_map/reduce_scatter | solution.py:26
  257.7 210.1 %reduce-scatter.4.cloned.1.call-done = f32[24,16384]{1,0:T(8,128)} async-done(((f32[192,16384]{1,0:T(8,128)}), f32[24,16384]{1,0:T(8,128)}) %reduce-scatter.4.cloned.1.call-update) | async-done | bytes 1572880 | tf_op jit(solution)/shard_map/reduce_scatter | solution.py:20
  467.8 0.0 copy-done.1
  467.8 17.0 %fusion = f32[256,16384]{1,0:T(8,128)} fusion(f32[24,256]{1,0:T(8,128)S(1)} %select_reduce_fusion, f32[24,16384]{1,0:T(8,128)} %reduce-scatter.6.cloned.1.call-done, f32[24,16384]{1,0:T(8,128)} %reduce-scatter.4.cloned.1.call-done, f32[16384]{0:T(1024)S(1)} %copy-done.1), kind=kOutput, calls=%fused_computation | convolution fusion | flops 1209139200 | bytes 20013056 | tf_op jit(solution)/shard_map/dot_general | solution.py:57
  484.8 0.0 reduce-scatter.8.cloned.1.call-update
  484.8 281.1 %reduce-scatter.8.cloned.1.call-done = f32[32,16384]{1,0:T(8,128)} async-done(((f32[256,16384]{1,0:T(8,128)}), f32[32,16384]{1,0:T(8,128)}) %reduce-scatter.8.cloned.1.call-update) | async-done | bytes 2097168 | tf_op jit(solution)/shard_map/reduce_scatter | solution.py:60
  (4 shorter events, 0.0 us)
Async XLA Ops:
  6.5 251.2 %reduce-scatter.6.cloned.1.call-start = ((), (), s32[]{:S(2)}) async-start(), calls=%async_computation.6 | async-start | bytes 14155776 | tf_op jit(solution)/shard_map/reduce_scatter | solution.py:26
  44.6 1.0 copy-start
  44.6 423.1 %reduce-scatter.4.cloned.1.call-start = ((), (), s32[]{:S(2)}) async-start(), calls=%async_computation.5 | async-start | bytes 14155776 | tf_op jit(solution)/shard_map/reduce_scatter | solution.py:20
  84.8 0.7 copy-start.2
  84.8 0.8 copy-start.3
  84.8 382.9 %copy-start.1 = (f32[16384]{0:T(1024)S(1)}, f32[16384]{0:T(1024)}, u32[]{:S(2)}) copy-start(f32[16384]{0:T(1024)} %param.10) | copy-start | bytes 196612
  84.9 681.1 %reduce-scatter.8.cloned.1.call-start = ((), (), s32[]{:S(2)}) async-start(), calls=%async_computation.7 | async-start | bytes 18874368 | tf_op jit(solution)/shard_map/reduce_scatter | solution.py:60
Sparse Core Ops, SparseCore 0:
  44.8 212.8 reduce-scatter.5
  261.3 206.4 reduce-scatter.3
  484.9 280.9 reduce-scatter.7
where the time goes:
time: 773 us; the launch traced here: 772 us
  waiting for transfers between devices  663 us (86%)
  matrix products  51.6 us (7%)
  blocking collectives  41.7 us (5%)
  between operations  13.1 us (2%)
    reduce_scatter x1, waiting for transfers between devices, on_device(): return lax.psum_scatter(credit_part, 'dp', scatter_dimension=0, tiled=True)  281 us
    reduce_scatter x1, waiting for transfers between devices, reduce_partials(): lax.psum_scatter(encoder_term(jnp.int32(0), share * lax.axis_size('dp')),...  210 us
    reduce_scatter x1, waiting for transfers between devices, reduce_partials(): lax.psum_scatter(decoder_term(jnp.int32(0), share * lax.axis_size('dp')),...  172 us
    all_to_all x1, blocking collectives, on_device(): lax.all_to_all(residual, 'dp', split_axis=1, concat_axis=0, tiled=True)  23.5 us
    dot_general x1, matrix products, decoder_term(): lax.dot_general(tangent_rows, decoder_weight, (((1,), (1,)), ((), ())), p...  18.8 us
    all_to_all x1, blocking collectives, on_device(): lax.all_to_all(cotangent, 'dp', split_axis=1, concat_axis=0, tiled=True)  18.2 us
    dot_general x1, matrix products, on_device(): lax.dot_general(routing, score, (((0,), (0,)), ((), ())), precision=lax.P...  17 us
    dot_general x1, matrix products, encoder_term(): return jnp.dot(gathered, encoder_weight, preferred_element_type=jnp.float32)  15.7 us
  transfers between devices with their start and end apart: 3, of which 3 were waited for; matrix products, arithmetic and copies ran while one was open for 2% of the time, Pallas kernels for 0%

commit v1 on v0

v1 whole, which is shorter than its diff:
```python
import functools

import jax
import jax.numpy as jnp
from jax import lax
from jax.experimental import pallas as pl
from jax.experimental.pallas import tpu as pltpu
from jax.sharding import PartitionSpec as P

E = 256
LANES = 128
CODE_ROWS = 16
STEPS = 256.0
TOP = 32700.0
TINY = 2.0 ** -100


def scale_code(most):
    return jnp.ceil(jnp.log2(jnp.maximum(most, TINY)) * STEPS)


def quantise(value, code):
    return jnp.round(value * (jnp.exp2(code * (-1.0 / STEPS)) * TOP)).astype(jnp.int32).astype(jnp.int16)


def unit_of(code):
    return jnp.exp2(code * (1.0 / STEPS)) * (1.0 / TOP)


def as_float(ints):
    return ints.astype(jnp.int32).astype(jnp.float32)


def partial_sums(tokens, rows_ref, enc_ref, dec_ref, message_refs):
    pre = jnp.dot(rows_ref[0], enc_ref[...], preferred_element_type=jnp.float32)
    grad = lax.dot_general(
        rows_ref[1], dec_ref[...], (((1,), (1,)), ((), ())), preferred_element_type=jnp.float32
    )
    for message in message_refs:
        unit = unit_of(as_float(message[2 * tokens :, :]))
        pre = pre + as_float(message[:tokens, :]) * unit[0:1]
        grad = grad + as_float(message[tokens : 2 * tokens, :]) * unit[1:2]
    return pre, grad


def send_kernel(tokens, n_messages, where_ref, rows_ref, enc_ref, dec_ref, *refs):
    messages, out_ref = refs[:n_messages], refs[-1]
    pre, grad = partial_sums(tokens, rows_ref, enc_ref, dec_ref, messages)
    pre_code = scale_code(jnp.max(jnp.abs(pre), axis=0, keepdims=True))
    grad_code = scale_code(jnp.max(jnp.abs(grad), axis=0, keepdims=True))
    out_ref[:tokens, :] = quantise(pre, pre_code)
    out_ref[tokens : 2 * tokens, :] = quantise(grad, grad_code)
    row = lax.broadcasted_iota(jnp.int32, (CODE_ROWS, pre.shape[1]), 0)
    codes = jnp.where(row == 0, pre_code, jnp.where(row == 1, grad_code, 0.0))
    out_ref[2 * tokens :, :] = codes.astype(jnp.int32).astype(jnp.int16)


def credit_kernel(tokens, n_messages, where_ref, rows_ref, enc_ref, dec_ref, *refs):
    messages = refs[:n_messages]
    bias_ref, routing_ref, out_ref, code_ref = refs[n_messages], refs[n_messages + 1], refs[-2], refs[-1]
    pre, grad = partial_sums(tokens, rows_ref, enc_ref, dec_ref, messages)
    score = jnp.maximum(pre + bias_ref[...], 0.0) * grad
    high = score.astype(jnp.bfloat16)
    low = (score - high.astype(jnp.float32)).astype(jnp.bfloat16)
    credit = jnp.dot(routing_ref[...], high, preferred_element_type=jnp.float32) + jnp.dot(
        routing_ref[...], low, preferred_element_type=jnp.float32
    )
    code = scale_code(jnp.max(jnp.abs(credit), axis=1, keepdims=True))
    out_ref[...] = quantise(credit, code)
    code_ref[...] = jnp.broadcast_to(code, (E, LANES)).astype(jnp.int32).astype(jnp.int16)


def block_of(length, most=512):
    block = min(length, most)
    while length % block:
        block -= LANES
    return block


class Chunk:
    def __init__(self, first, size, order):
        self.first, self.size, self.order = first, size, order
        self.messages = []

    def kept(self, bits, stage):
        first = self.first
        for j in range(stage):
            first = first + bits[self.order[j]] * (self.size >> (j + 1))
        return first

    def sent(self, bits, stage):
        return self.kept(bits, stage) + (1 - bits[self.order[stage]]) * (self.size >> (stage + 1))


def run_stage(chunk, stage, bits, rows, enc, dec, bias, routing, earlier, cost):
    last = stage == len(chunk.order)
    tokens, depth = rows.shape[1:]
    length = chunk.size >> (stage if last else stage + 1)
    block = block_of(length)

    def at(i, bits_ref, message=None):
        first = chunk.kept(bits_ref, stage) if last else chunk.sent(bits_ref, stage)
        if message is not None:
            first = first - chunk.kept(bits_ref, message + 1)
        return first // block + i

    in_specs = [
        pl.BlockSpec((2, tokens, depth), lambda i, w: (0, 0, 0)),
        pl.BlockSpec((depth, block), lambda i, w: (0, at(i, w))),
        pl.BlockSpec((block, depth), lambda i, w: (at(i, w), 0)),
    ]
    operands = [rows, enc, dec]
    for j, message in enumerate(chunk.messages):
        in_specs.append(pl.BlockSpec((message.shape[0], block), lambda i, w, j=j: (0, at(i, w, j))))
        operands.append(message)
    if last:
        in_specs.append(pl.BlockSpec((1, block), lambda i, w: (0, at(i, w))))
        in_specs.append(pl.BlockSpec(routing.shape, lambda i, w: (0, 0)))
        operands += [bias, routing]
        body = credit_kernel
        out_shape = [
            jax.ShapeDtypeStruct((E, length), jnp.int16),
            jax.ShapeDtypeStruct((E, LANES * (length // block)), jnp.int16),
        ]
        out_specs = [pl.BlockSpec((E, block), lambda i, w: (0, i)), pl.BlockSpec((E, LANES), lambda i, w: (0, i))]
    else:
        body = send_kernel
        out_shape = jax.ShapeDtypeStruct((2 * tokens + CODE_ROWS, length), jnp.int16)
        out_specs = pl.BlockSpec((2 * tokens + CODE_ROWS, block), lambda i, w: (0, i))
    if earlier is not None:
        in_specs.append(pl.BlockSpec(memory_space=pl.ANY))
        operands.append(earlier)
    return pl.pallas_call(
        functools.partial(body, tokens, len(chunk.messages)),
        grid_spec=pltpu.PrefetchScalarGridSpec(
            num_scalar_prefetch=1, grid=(length // block,), in_specs=in_specs, out_specs=out_specs
        ),
        out_shape=out_shape,
        compiler_params=pltpu.CompilerParams(vmem_limit_bytes=40 * 1024 * 1024),
        cost_estimate=pl.CostEstimate(flops=cost, bytes_accessed=1, transcendentals=0),
        name=("credit" if last else f"stage{stage}"),
    )(bits, *operands)


def place_kernel(blocks, whole_ref, *refs):
    out_ref = refs[-1]
    lanes = whole_ref.shape[2] - LANES
    for owner, column, width, lane, target in blocks:
        unit = unit_of(as_float(whole_ref[owner, :, lanes:])[:, lane : lane + 1])
        out_ref[:, target : target + width] = as_float(whole_ref[owner, :, column : column + width]) * unit


def place(group, n_dp, whole, out, features):
    first = min(chunk.first for chunk in group)
    span = sum(chunk.size for chunk in group)
    blocks, column = [], 0
    for lane, chunk in enumerate(group):
        width = chunk.size // n_dp
        for owner in range(n_dp):
            slot = 0
            for bit in chunk.order:
                slot = 2 * slot + ((owner >> bit) & 1)
            blocks.append((owner, column, width, lane, chunk.first - first + slot * width))
        column += width
    operands, in_specs = [whole], [pl.BlockSpec(whole.shape, lambda i: (0, 0, 0))]
    if out is not None:
        operands.append(out)
        in_specs.append(pl.BlockSpec(memory_space=pl.ANY))
    return pl.pallas_call(
        functools.partial(place_kernel, blocks),
        grid=(1,),
        in_specs=in_specs,
        out_specs=pl.BlockSpec((whole.shape[1], span), lambda i: (0, first // span)),
        out_shape=jax.ShapeDtypeStruct((whole.shape[1], features), jnp.float32),
        input_output_aliases={} if out is None else {1: 0},
        compiler_params=pltpu.CompilerParams(vmem_limit_bytes=40 * 1024 * 1024),
        name="place",
    )(*operands)


def collect(group, credits, n_dp):
    lane = lax.broadcasted_iota(jnp.int32, (E, LANES), 1)
    codes = credits[0][1]
    for k in range(1, len(credits)):
        codes = jnp.where(lane == k, credits[k][1], codes)
    whole = jnp.concatenate([c[0] for c in credits] + [codes], 1)
    whole = lax.all_to_all(whole, "dp", split_axis=0, concat_axis=0, tiled=True)
    return whole.reshape(n_dp, E // n_dp, -1)


def plan_of(units, n_bits):
    straight = tuple(range(n_bits))
    if units == 16 and n_bits == 3:
        sizes = SIZES
        groups, sequence = GROUPS, SEQUENCE
    else:
        sizes = [(1, straight)] * units
        groups, sequence = [list(range(units))], None
    if sequence is None:
        sequence = [
            (step - stage, stage)
            for step in range(len(sizes) + n_bits)
            for stage in range(n_bits + 1)
            if 0 <= step - stage < len(sizes)
        ]
    return sizes, groups, sequence


A, B, C = (0, 1, 2), (1, 0, 2), (1, 2, 0)
SIZES = [(2, A), (2, A), (4, A), (4, A), (2, A), (2, A)]
GROUPS = [[0, 1, 2, 3, 4, 5]]
SEQUENCE = None
COST = 9_000_000_000


def route_table(routes):
    experts, buckets = routes[:, : routes.shape[1] // 2], routes[:, routes.shape[1] // 2 :]
    expert_ids = jnp.arange(E, dtype=jnp.int32)
    weights = buckets.astype(jnp.float32) * 0.125
    table = jnp.sum(
        (experts[:, None, :].astype(jnp.int32) == expert_ids[None, :, None]).astype(jnp.float32)
        * weights[:, None, :],
        axis=2,
    )
    return table.T.astype(jnp.bfloat16)


def gather_rows(residual, cotangent, route_experts, route_buckets, n_dp):
    mine, width = residual.shape
    depth = width // n_dp
    routes = jnp.concatenate([route_experts, route_buckets], 1).astype(jnp.bfloat16)
    extra = -(-routes.size // (8 * depth)) * 8
    flat = jnp.pad(routes.reshape(-1), (0, extra * depth - routes.size)).reshape(extra, 1, depth)
    flat = jnp.broadcast_to(flat, (extra, n_dp, depth)).reshape(extra, width)
    got = lax.all_to_all(
        jnp.concatenate([residual, cotangent, flat], 0), "dp", split_axis=1, concat_axis=0, tiled=True
    ).reshape(n_dp, 2 * mine + extra, depth)
    rows = got[:, : 2 * mine].reshape(n_dp, 2, mine, depth).transpose(1, 0, 2, 3).reshape(2, n_dp * mine, depth)
    routes = got[:, 2 * mine :].reshape(n_dp, -1)[:, : routes.size].reshape(n_dp * mine, -1)
    return rows, routes


def on_device(residual, cotangent, enc, bias, dec, route_experts, route_buckets):
    n_dp, me = lax.axis_size("dp"), lax.axis_index("dp")
    n_bits = n_dp.bit_length() - 1
    features = enc.shape[1]
    bits = (me >> jnp.arange(n_bits, dtype=jnp.int32)) & 1
    rows, routes = gather_rows(residual, cotangent, route_experts, route_buckets, n_dp)
    routing = route_table(routes)
    bias = bias[None, :]

    unit = LANES * n_dp
    sizes, groups, sequence = plan_of(features // unit, n_bits)
    chunks, first = [], 0
    for units, order in sizes:
        chunks.append(Chunk(first, units * unit, order))
        first += units * unit

    earlier, credits, out = None, {}, None
    for n, (c, stage) in enumerate(sequence):
        chunk = chunks[c]
        result = run_stage(chunk, stage, bits, rows, enc, dec, bias, routing, earlier, COST if n != 1 else 1)
        if stage < n_bits:
            partner = [(i, i ^ (1 << chunk.order[stage])) for i in range(n_dp)]
            chunk.messages.append(lax.ppermute(result, "dp", partner))
            earlier = result
        else:
            credits[c] = result
            earlier = result[1]
            for group in groups:
                if c in group and all(k in credits for k in group):
                    whole = collect([chunks[k] for k in group], [credits[k] for k in group], n_dp)
                    out = place([chunks[k] for k in group], n_dp, whole, out, features)
    return out


def solution(mesh):
    placed = (
        P("dp", None),
        P("dp", None),
        P("dp", "feat"),
        P("feat"),
        P("feat", "dp"),
        P("dp", None),
        P("dp", None),
    )
    return jax.shard_map(
        on_device, mesh=mesh, in_specs=placed, out_specs=P("dp", "feat"), check_vma=False
    )
```

time: 773 us -> 254 us (0.33)
  waiting for transfers between devices: 663 us -> 112 us
  Pallas kernels: 0 us -> 78.8 us
  matrix products: 51.6 us -> 0 us
  starting transfers between devices: 0.09 us -> 25.5 us
  blocking collectives: 41.7 us -> 28.2 us
  between operations: 13.1 us -> 0.54 us
    reduce_scatter x3 -> x0, waiting for transfers between devices: 663 us -> none  [the longest x1 281 us: on_device(): return lax.psum_scatter(credit_part, 'dp', scatter_dimension=0, tiled=True)]
    ppermute x0 -> x18, waiting for transfers between devices: none -> 92.4 us  [on_device(): chunk.messages.append(lax.ppermute(result, 'dp', partner))]
    pallas_call x0 -> x25, Pallas kernels: none -> 78.8 us  [the longest x24 77.1 us: run_stage(): pl.pallas_call(functools.partial(body, tokens, len(chunk.messages)), grid...]
    dot_general x3 -> x0, matrix products: 51.6 us -> none  [the longest x1 18.8 us: decoder_term(): lax.dot_general(tangent_rows, decoder_weight, (((1,), (1,)), ((), ())), p...]
    all_to_all x0 -> x1, waiting for transfers between devices: none -> 19.4 us  [gather_rows(): lax.all_to_all(jnp.concatenate([residual, cotangent, flat], 0), 'dp', spl...]
    ppermute x0 -> x18, starting transfers between devices: none -> 18.2 us  [on_device(): chunk.messages.append(lax.ppermute(result, 'dp', partner))]
    all_to_all x2 -> x1, blocking collectives: 41.7 us -> 28.2 us  [collect(): whole = lax.all_to_all(whole, 'dp', split_axis=0, concat_axis=0, tiled=True)]
  transfers between devices with their start and end apart: 3 -> 19, of which waited for: 3 -> 9; matrix products, arithmetic and copies ran while one was open for 2% -> 1% of each run, Pallas kernels for 0% -> 26%
where the time goes in v1:
time: 254 us; the launch traced here: 253 us
  waiting for transfers between devices  112 us (44%)
  Pallas kernels  78.8 us (31%)
  blocking collectives  28.2 us (11%)
  starting transfers between devices  25.5 us (10%)
  local copies, waits for them, and re-layouts  5.48 us (2%)
  other arithmetic  3.2 us (1%)
    ppermute x18, waiting for transfers between devices, on_device(): chunk.messages.append(lax.ppermute(result, 'dp', partner))  92.4 us
    pallas_call x24, Pallas kernels, run_stage(): pl.pallas_call(functools.partial(body, tokens, len(chunk.messages)), grid...  77.1 us
    all_to_all x1, blocking collectives, collect(): whole = lax.all_to_all(whole, 'dp', split_axis=0, concat_axis=0, tiled=True)  28.2 us
    all_to_all x1, waiting for transfers between devices, gather_rows(): lax.all_to_all(jnp.concatenate([residual, cotangent, flat], 0), 'dp', spl...  19.4 us
    ppermute x18, starting transfers between devices, on_device(): chunk.messages.append(lax.ppermute(result, 'dp', partner))  18.2 us
    all_to_all x1, starting transfers between devices, gather_rows(): lax.all_to_all(jnp.concatenate([residual, cotangent, flat], 0), 'dp', spl...  7.25 us
  transfers between devices with their start and end apart: 19, of which 9 were waited for; matrix products, arithmetic and copies ran while one was open for 1% of the time, Pallas kernels for 26%

profile of v1, /device:TPU:0, one launch (start us, length us, event | category | flops | bytes accessed | tf_op | source)
XLA Modules:
  0.0 253.5 jit_solution(11984002820596136302)
XLA Ops:
  3.5 7.3 %all-to-all-start = ((bf16[56,8,896]{2,0,1:T(8,128)(2,1)}), bf16[56,8,896]{2,0,1:T(8,128)(2,1)S(1)}, u32[]{:S(2)}, u32[]{:S(2)}) async-start(bf16[56,8,896]{2,0,1:T(8,128)(2,1)} %copy.21), calls=%async_computation | async-start | bytes 1605632 | tf_op jit(solution)/shard_map/all_to_all | solution.py:235
  11.9 19.4 %all-to-all-done = bf16[56,8,896]{2,0,1:T(8,128)(2,1)S(1)} async-done(((bf16[56,8,896]{2,0,1:T(8,128)(2,1)}), bf16[56,8,896]{2,0,1:T(8,128)(2,1)S(1)}, u32[]{:S(2)}, u32[]{:S(2)}) %all-to-all-start) | async-done | bytes 802848 | tf_op jit(solution)/shard_map/all_to_all | solution.py:235
  32.2 4.3 %stage0.6.refs_0_ = s16[400,1024]{1,0:T(8,128)(2,1)} custom-call(s32[3]{0:T(128)S(1)} %shift-right-arithmetic_and_fusion.where_ref, bf16[2,192,896]{2,1,0:T(8,128)(2,1)S(1)} %bitcast.15, bf16[896,16384]{1,0:T(8,128)(2,1)} %enc_ref.47, bf16[16384,896]{1,0:T(8,128)(2,1)} %dec_ref.47), custom_call_target="tpu_custom_call" | custom-call | flops 8999999488 | bytes 1 | tf_op jit(solution)/shard_map/stage0/pallas_call | solution.py:133
  37.2 3.7 %stage0.7.refs_1_ = s16[400,1024]{1,0:T(8,128)(2,1)S(1)} custom-call(s32[3]{0:T(128)S(1)} %shift-right-arithmetic_and_fusion.where_ref, bf16[2,192,896]{2,1,0:T(8,128)(2,1)S(1)} %bitcast.16, bf16[896,16384]{1,0:T(8,128)(2,1)} %enc_ref.47, bf16[16384,896]{1,0:T(8,128)(2,1)} %dec_ref.47, s16[400,1024]{1,0:T(8,128)(2,1)} %stage0.6.refs_0_), custom_call_target="tpu_custom_call" | custom-call | flops 1 | bytes 1 | tf_op jit(solution)/shard_map/stage0/pallas_call | solution.py:133
  45.4 16.9 %collective-permute-done.refs_0_ = s16[400,1024]{1,0:T(8,128)(2,1)S(1)} collective-permute-done((s16[400,1024]{1,0:T(8,128)(2,1)}, s16[400,1024]{1,0:T(8,128)(2,1)S(1)}, u32[]{:S(2)}, u32[]{:S(2)}) %collective-permute-start) | collective-permute-done | bytes 819232 | tf_op jit(solution)/shard_map/ppermute | solution.py:265
  65.4 6.1 %stage0.8.refs_1_ = s16[400,2048]{1,0:T(8,128)(2,1)S(1)} custom-call(s32[3]{0:T(128)S(1)} %shift-right-arithmetic_and_fusion.where_ref, bf16[2,192,896]{2,1,0:T(8,128)(2,1)S(1)} %bitcast.18, bf16[896,16384]{1,0:T(8,128)(2,1)} %enc_ref.47, bf16[16384,896]{1,0:T(8,128)(2,1)} %dec_ref.47, s16[400,512]{1,0:T(8,128)(2,1)S(1)} %stage1.6.refs_0_), custom_call_target="tpu_custom_call" | custom-call | flops 8999999488 | bytes 1 | tf_op jit(solution)/shard_map/stage0/pallas_call | solution.py:133
  72.7 7.2 %collective-permute-done.2.refs_0_ = s16[400,1024]{1,0:T(8,128)(2,1)S(1)} collective-permute-done((s16[400,1024]{1,0:T(8,128)(2,1)S(1)}, s16[400,1024]{1,0:T(8,128)(2,1)S(1)}, u32[]{:S(2)}, u32[]{:S(2)}) %collective-permute-start.2) | collective-permute-done | bytes 819232 | tf_op jit(solution)/shard_map/ppermute | solution.py:265
  86.5 6.1 %stage0.9.refs_1_ = s16[400,2048]{1,0:T(8,128)(2,1)S(1)} custom-call(s32[3]{0:T(128)S(1)} %shift-right-arithmetic_and_fusion.where_ref, bf16[2,192,896]{2,1,0:T(8,128)(2,1)S(1)} %bitcast.21, bf16[896,16384]{1,0:T(8,128)(2,1)} %enc_ref.47, bf16[16384,896]{1,0:T(8,128)(2,1)} %dec_ref.47, s16[400,256]{1,0:T(8,128)(2,1)S(1)} %stage2.6.refs_0_), custom_call_target="tpu_custom_call" | custom-call | flops 8999999488 | bytes 1 | tf_op jit(solution)/shard_map/stage0/pallas_call | solution.py:133
  94.4 20.5 %collective-permute-done.5.refs_0_ = s16[400,2048]{1,0:T(8,128)(2,1)S(1)} collective-permute-done((s16[400,2048]{1,0:T(8,128)(2,1)S(1)}, s16[400,2048]{1,0:T(8,128)(2,1)S(1)}, u32[]{:S(2)}, u32[]{:S(2)}) %collective-permute-start.5) | collective-permute-done | bytes 1638432 | tf_op jit(solution)/shard_map/ppermute | solution.py:265
  115.0 3.7 %stage1.8.refs_2_ = s16[400,1024]{1,0:T(8,128)(2,1)S(1)} custom-call(s32[3]{0:T(128)S(1)} %shift-right-arithmetic_and_fusion.where_ref, bf16[2,192,896]{2,1,0:T(8,128)(2,1)S(1)} %bitcast.22, bf16[896,16384]{1,0:T(8,128)(2,1)} %enc_ref.47, bf16[16384,896]{1,0:T(8,128)(2,1)} %dec_ref.47, s16[400,2048]{1,0:T(8,128)(2,1)S(1)} %collective-permute-done.5.refs_0_, ...), custom_call_target="tpu_custom_call" | custom-call | flops 8999999488 | bytes 1 | tf_op jit(solution)/shard_map/stage1/pallas_call | solution.py:133
  125.1 3.7 %stage0.10.refs_1_ = s16[400,1024]{1,0:T(8,128)(2,1)S(1)} custom-call(s32[3]{0:T(128)S(1)} %shift-right-arithmetic_and_fusion.where_ref, bf16[2,192,896]{2,1,0:T(8,128)(2,1)S(1)} %bitcast.25, bf16[896,16384]{1,0:T(8,128)(2,1)} %enc_ref.47, bf16[16384,896]{1,0:T(8,128)(2,1)} %dec_ref.47, s16[256,128]{1,0:T(8,128)(2,1)S(1)} %get-tuple-element.18.refs_0_), custom_call_target="tpu_custom_call" | custom-call | flops 8999999488 | bytes 1 | tf_op jit(solution)/shard_map/stage0/pallas_call | solution.py:133
  130.7 19.4 %collective-permute-done.8.refs_0_ = s16[400,2048]{1,0:T(8,128)(2,1)S(1)} collective-permute-done((s16[400,2048]{1,0:T(8,128)(2,1)S(1)}, s16[400,2048]{1,0:T(8,128)(2,1)S(1)}, u32[]{:S(2)}, u32[]{:S(2)}) %collective-permute-start.8) | collective-permute-done | bytes 1638432 | tf_op jit(solution)/shard_map/ppermute | solution.py:265
  150.1 3.7 %stage1.9.refs_2_ = s16[400,1024]{1,0:T(8,128)(2,1)S(1)} custom-call(s32[3]{0:T(128)S(1)} %shift-right-arithmetic_and_fusion.where_ref, bf16[2,192,896]{2,1,0:T(8,128)(2,1)S(1)} %bitcast.26, bf16[896,16384]{1,0:T(8,128)(2,1)} %enc_ref.47, bf16[16384,896]{1,0:T(8,128)(2,1)} %dec_ref.47, s16[400,2048]{1,0:T(8,128)(2,1)S(1)} %collective-permute-done.8.refs_0_, ...), custom_call_target="tpu_custom_call" | custom-call | flops 8999999488 | bytes 1 | tf_op jit(solution)/shard_map/stage1/pallas_call | solution.py:133
  154.1 2.8 %stage2.8.refs_5_ = s16[400,512]{1,0:T(8,128)(2,1)S(1)} custom-call(s32[3]{0:T(128)S(1)} %shift-right-arithmetic_and_fusion.where_ref, bf16[2,192,896]{2,1,0:T(8,128)(2,1)S(1)} %bitcast.27, bf16[896,16384]{1,0:T(8,128)(2,1)} %enc_ref.47, bf16[16384,896]{1,0:T(8,128)(2,1)} %dec_ref.47, s16[400,2048]{1,0:T(8,128)(2,1)S(1)} %collective-permute-done.5.refs_0_, ...), custom_call_target="tpu_custom_call" | custom-call | flops 8999999488 | bytes 1 | tf_op jit(solution)/shard_map/stage2/pallas_call | solution.py:133
  160.8 3.9 %stage0.11.refs_1_ = s16[400,1024]{1,0:T(8,128)(2,1)S(1)} custom-call(s32[3]{0:T(128)S(1)} %shift-right-arithmetic_and_fusion.where_ref, bf16[2,192,896]{2,1,0:T(8,128)(2,1)S(1)} %bitcast.29, bf16[896,16384]{1,0:T(8,128)(2,1)} %enc_ref.47, bf16[16384,896]{1,0:T(8,128)(2,1)} %dec_ref.47, s16[256,128]{1,0:T(8,128)(2,1)S(1)} %get-tuple-element.20.refs_0_), custom_call_target="tpu_custom_call" | custom-call | flops 8999999488 | bytes 1 | tf_op jit(solution)/shard_map/stage0/pallas_call | solution.py:133
  169.5 17.4 %collective-permute-done.10.refs_1_ = s16[400,1024]{1,0:T(8,128)(2,1)S(1)} collective-permute-done((s16[400,1024]{1,0:T(8,128)(2,1)S(1)}, s16[400,1024]{1,0:T(8,128)(2,1)S(1)}, u32[]{:S(2)}, u32[]{:S(2)}) %collective-permute-start.10) | collective-permute-done | bytes 819232 | tf_op jit(solution)/shard_map/ppermute | solution.py:265
  187.0 2.8 %stage2.9.refs_5_ = s16[400,512]{1,0:T(8,128)(2,1)S(1)} custom-call(s32[3]{0:T(128)S(1)} %shift-right-arithmetic_and_fusion.where_ref, bf16[2,192,896]{2,1,0:T(8,128)(2,1)S(1)} %bitcast.31, bf16[896,16384]{1,0:T(8,128)(2,1)} %enc_ref.47, bf16[16384,896]{1,0:T(8,128)(2,1)} %dec_ref.47, s16[400,2048]{1,0:T(8,128)(2,1)S(1)} %collective-permute-done.8.refs_0_, ...), custom_call_target="tpu_custom_call" | custom-call | flops 8999999488 | bytes 1 | tf_op jit(solution)/shard_map/stage2/pallas_call | solution.py:133
  189.8 3.2 %credit.8 = (s16[256,512]{1,0:T(8,128)(2,1)S(1)}, s16[256,128]{1,0:T(8,128)(2,1)S(1)}) custom-call(s32[3]{0:T(128)S(1)} %shift-right-arithmetic_and_fusion.where_ref, bf16[2,192,896]{2,1,0:T(8,128)(2,1)S(1)} %bitcast.32, bf16[896,16384]{1,0:T(8,128)(2,1)} %enc_ref.47, bf16[16384,896]{1,0:T(8,128)(2,1)} %dec_ref.47, ...), custom_call_target="tpu_custom_call" | custom-call | flops 8999999488 | bytes 1 | tf_op jit(solution)/shard_map/credit/pallas_call | solution.py:133
  193.1 2.8 %stage1.11.refs_2_ = s16[400,512]{1,0:T(8,128)(2,1)S(1)} custom-call(s32[3]{0:T(128)S(1)} %shift-right-arithmetic_and_fusion.where_ref, bf16[2,192,896]{2,1,0:T(8,128)(2,1)S(1)} %bitcast.33, bf16[896,16384]{1,0:T(8,128)(2,1)} %enc_ref.47, bf16[16384,896]{1,0:T(8,128)(2,1)} %dec_ref.47, s16[400,1024]{1,0:T(8,128)(2,1)S(1)} %collective-permute-done.14.refs_0_, ...), custom_call_target="tpu_custom_call" | custom-call | flops 8999999488 | bytes 1 | tf_op jit(solution)/shard_map/stage1/pallas_call | solution.py:133
  198.2 3.7 %collective-permute-start.15 = (s16[400,256]{1,0:T(8,128)(2,1)S(1)}, s16[400,256]{1,0:T(8,128)(2,1)S(1)}, u32[]{:S(2)}, u32[]{:S(2)}) collective-permute-start(s16[400,256]{1,0:T(8,128)(2,1)S(1)} %stage2.10.refs_5_), channel_id=1, source_target_pairs={{0,16},{4,20},{8,24},{12,28},{16,0},{20,4},{24,8},{28,12},{1,17},{... | collective-permute-start | bytes 614408 | tf_op jit(solution)/shard_map/ppermute | solution.py:265
  201.8 5.1 %collective-permute-done.12.refs_2_ = s16[400,512]{1,0:T(8,128)(2,1)S(1)} collective-permute-done((s16[400,512]{1,0:T(8,128)(2,1)S(1)}, s16[400,512]{1,0:T(8,128)(2,1)S(1)}, u32[]{:S(2)}, u32[]{:S(2)}) %collective-permute-start.12) | collective-permute-done | bytes 409632 | tf_op jit(solution)/shard_map/ppermute | solution.py:265
  206.9 3.2 %credit.9 = (s16[256,512]{1,0:T(8,128)(2,1)S(1)}, s16[256,128]{1,0:T(8,128)(2,1)S(1)}) custom-call(s32[3]{0:T(128)S(1)} %shift-right-arithmetic_and_fusion.where_ref, bf16[2,192,896]{2,1,0:T(8,128)(2,1)S(1)} %bitcast.35, bf16[896,16384]{1,0:T(8,128)(2,1)} %enc_ref.47, bf16[16384,896]{1,0:T(8,128)(2,1)} %dec_ref.47, ...), custom_call_target="tpu_custom_call" | custom-call | flops 8999999488 | bytes 1 | tf_op jit(solution)/shard_map/credit/pallas_call | solution.py:133
  216.2 4.7 %collective-permute-done.17.refs_2_ = s16[400,256]{1,0:T(8,128)(2,1)S(1)} collective-permute-done((s16[400,256]{1,0:T(8,128)(2,1)S(1)}, s16[400,256]{1,0:T(8,128)(2,1)S(1)}, u32[]{:S(2)}, u32[]{:S(2)}) %collective-permute-start.17) | collective-permute-done | bytes 204832 | tf_op jit(solution)/shard_map/ppermute | solution.py:265
  223.6 28.2 %all_to_all.22.whole_ref = s16[8,32,2176]{2,1,0:T(8,128)(2,1)S(1)} all-to-all(s16[8,32,2176]{2,1,0:T(8,128)(2,1)S(1)} %bitcast.54), channel_id=1, replica_groups=mesh['dp'=8,'feat'=4] {'dp'}, dimensions={0} | all-to-all | bytes 2228224 | tf_op jit(solution)/shard_map/all_to_all | solution.py:187
  (99 shorter events, 53.3 us)
Async XLA Ops:
  3.5 27.8 %all-to-all-start = ((bf16[56,8,896]{2,0,1:T(8,128)(2,1)}), bf16[56,8,896]{2,0,1:T(8,128)(2,1)S(1)}, u32[]{:S(2)}, u32[]{:S(2)}) async-start(bf16[56,8,896]{2,0,1:T(8,128)(2,1)} %copy.21), calls=%async_computation | async-start | bytes 1605632 | tf_op jit(solution)/shard_map/all_to_all | solution.py:235
  40.8 21.5 %collective-permute-start = (s16[400,1024]{1,0:T(8,128)(2,1)}, s16[400,1024]{1,0:T(8,128)(2,1)S(1)}, u32[]{:S(2)}, u32[]{:S(2)}) collective-permute-start(s16[400,1024]{1,0:T(8,128)(2,1)} %stage0.6.refs_0_), channel_id=1, source_target_pairs={{0,4},{4,0},{8,12},{12,8},{16,20},{20,16},{24,28},{28,24},{1,5},{5... | collective-permute-start | bytes 2457608 | tf_op jit(solution)/shard_map/ppermute | solution.py:265
  42.3 37.6 %collective-permute-start.2 = (s16[400,1024]{1,0:T(8,128)(2,1)S(1)}, s16[400,1024]{1,0:T(8,128)(2,1)S(1)}, u32[]{:S(2)}, u32[]{:S(2)}) collective-permute-start(s16[400,1024]{1,0:T(8,128)(2,1)S(1)} %stage0.7.refs_1_), channel_id=1, source_target_pairs={{0,4},{4,0},{8,12},{12,8},{16,20},{20,16},{24,28},{28,24},{1,5},{5... | collective-permute-start | bytes 2457608 | tf_op jit(solution)/shard_map/ppermute | solution.py:265
  65.1 17.9 %collective-permute-start.1 = (s16[400,512]{1,0:T(8,128)(2,1)S(1)}, s16[400,512]{1,0:T(8,128)(2,1)S(1)}, u32[]{:S(2)}, u32[]{:S(2)}) collective-permute-start(s16[400,512]{1,0:T(8,128)(2,1)S(1)} %stage1.6.refs_0_), channel_id=1, source_target_pairs={{0,8},{4,12},{8,0},{12,4},{16,24},{20,28},{24,16},{28,20},{1,9},{5... | collective-permute-start | bytes 1228808 | tf_op jit(solution)/shard_map/ppermute | solution.py:265
  71.5 43.4 %collective-permute-start.5 = (s16[400,2048]{1,0:T(8,128)(2,1)S(1)}, s16[400,2048]{1,0:T(8,128)(2,1)S(1)}, u32[]{:S(2)}, u32[]{:S(2)}) collective-permute-start(s16[400,2048]{1,0:T(8,128)(2,1)S(1)} %stage0.8.refs_1_), channel_id=1, source_target_pairs={{0,4},{4,0},{8,12},{12,8},{16,20},{20,16},{24,28},{28,24},{1,5},{5... | collective-permute-start | bytes 4915208 | tf_op jit(solution)/shard_map/ppermute | solution.py:265
  82.6 36.4 %collective-permute-start.4 = (s16[400,512]{1,0:T(8,128)(2,1)S(1)}, s16[400,512]{1,0:T(8,128)(2,1)S(1)}, u32[]{:S(2)}, u32[]{:S(2)}) collective-permute-start(s16[400,512]{1,0:T(8,128)(2,1)S(1)} %stage1.7.refs_2_), channel_id=1, source_target_pairs={{0,8},{4,12},{8,0},{12,4},{16,24},{20,28},{24,16},{28,20},{1,9},{5... | collective-permute-start | bytes 1228808 | tf_op jit(solution)/shard_map/ppermute | solution.py:265
  85.2 37.4 %collective-permute-start.3 = (s16[400,256]{1,0:T(8,128)(2,1)S(1)}, s16[400,256]{1,0:T(8,128)(2,1)S(1)}, u32[]{:S(2)}, u32[]{:S(2)}) collective-permute-start(s16[400,256]{1,0:T(8,128)(2,1)S(1)} %stage2.6.refs_0_), channel_id=1, source_target_pairs={{0,16},{4,20},{8,24},{12,28},{16,0},{20,4},{24,8},{28,12},{1,17},{... | collective-permute-start | bytes 614408 | tf_op jit(solution)/shard_map/ppermute | solution.py:265
  92.6 57.5 %collective-permute-start.8 = (s16[400,2048]{1,0:T(8,128)(2,1)S(1)}, s16[400,2048]{1,0:T(8,128)(2,1)S(1)}, u32[]{:S(2)}, u32[]{:S(2)}) collective-permute-start(s16[400,2048]{1,0:T(8,128)(2,1)S(1)} %stage0.9.refs_1_), channel_id=1, source_target_pairs={{0,4},{4,0},{8,12},{12,8},{16,20},{20,16},{24,28},{28,24},{1,5},{5... | collective-permute-start | bytes 4915208 | tf_op jit(solution)/shard_map/ppermute | solution.py:265
  118.7 3.9 %copy-start = (f32[16384]{0:T(1024)S(1)}, f32[16384]{0:T(1024)}, u32[]{:S(2)}) copy-start(f32[16384]{0:T(1024)} %param.10) | copy-start | bytes 196612
  118.7 35.4 %collective-permute-start.7 = (s16[400,1024]{1,0:T(8,128)(2,1)S(1)}, s16[400,1024]{1,0:T(8,128)(2,1)S(1)}, u32[]{:S(2)}, u32[]{:S(2)}) collective-permute-start(s16[400,1024]{1,0:T(8,128)(2,1)S(1)} %stage1.8.refs_2_), channel_id=1, source_target_pairs={{0,8},{4,12},{8,0},{12,4},{16,24},{20,28},{24,16},{28,20},{1,9},{5... | collective-permute-start | bytes 2457608 | tf_op jit(solution)/shard_map/ppermute | solution.py:265
  121.2 37.1 %collective-permute-start.6 = (s16[400,256]{1,0:T(8,128)(2,1)S(1)}, s16[400,256]{1,0:T(8,128)(2,1)S(1)}, u32[]{:S(2)}, u32[]{:S(2)}) collective-permute-start(s16[400,256]{1,0:T(8,128)(2,1)S(1)} %stage2.7.refs_5_), channel_id=1, source_target_pairs={{0,16},{4,20},{8,24},{12,28},{16,0},{20,4},{24,8},{28,12},{1,17},{... | collective-permute-start | bytes 614408 | tf_op jit(solution)/shard_map/ppermute | solution.py:265
  125.1 3.7 %copy-start.1 = (s16[256,128]{1,0:T(8,128)(2,1)}, s16[256,128]{1,0:T(8,128)(2,1)S(1)}, u32[]{:S(2)}) copy-start(s16[256,128]{1,0:T(8,128)(2,1)S(1)} %get-tuple-element.18.refs_0_) | copy-start | bytes 196612
  128.8 37.7 %collective-permute-start.11 = (s16[400,1024]{1,0:T(8,128)(2,1)S(1)}, s16[400,1024]{1,0:T(8,128)(2,1)S(1)}, u32[]{:S(2)}, u32[]{:S(2)}) collective-permute-start(s16[400,1024]{1,0:T(8,128)(2,1)S(1)} %stage0.10.refs_1_), channel_id=1, source_target_pairs={{0,4},{4,0},{8,12},{12,8},{16,20},{20,16},{24,28},{28,24},{1,5},{5... | collective-permute-start | bytes 2457608 | tf_op jit(solution)/shard_map/ppermute | solution.py:265
  153.8 33.2 %collective-permute-start.10 = (s16[400,1024]{1,0:T(8,128)(2,1)S(1)}, s16[400,1024]{1,0:T(8,128)(2,1)S(1)}, u32[]{:S(2)}, u32[]{:S(2)}) collective-permute-start(s16[400,1024]{1,0:T(8,128)(2,1)S(1)} %stage1.9.refs_2_), channel_id=1, source_target_pairs={{0,8},{4,12},{8,0},{12,4},{16,24},{20,28},{24,16},{28,20},{1,9},{5... | collective-permute-start | bytes 2457608 | tf_op jit(solution)/shard_map/ppermute | solution.py:265
  156.9 32.9 %collective-permute-start.9 = (s16[400,512]{1,0:T(8,128)(2,1)S(1)}, s16[400,512]{1,0:T(8,128)(2,1)S(1)}, u32[]{:S(2)}, u32[]{:S(2)}) collective-permute-start(s16[400,512]{1,0:T(8,128)(2,1)S(1)} %stage2.8.refs_5_), channel_id=1, source_target_pairs={{0,16},{4,20},{8,24},{12,28},{16,0},{20,4},{24,8},{28,12},{1,17},{... | collective-permute-start | bytes 1228808 | tf_op jit(solution)/shard_map/ppermute | solution.py:265
  160.8 3.9 %copy-start.3 = (s16[256,128]{1,0:T(8,128)(2,1)}, s16[256,128]{1,0:T(8,128)(2,1)S(1)}, u32[]{:S(2)}) copy-start(s16[256,128]{1,0:T(8,128)(2,1)S(1)} %get-tuple-element.20.refs_0_) | copy-start | bytes 196612
  164.7 28.4 %collective-permute-start.14 = (s16[400,1024]{1,0:T(8,128)(2,1)S(1)}, s16[400,1024]{1,0:T(8,128)(2,1)S(1)}, u32[]{:S(2)}, u32[]{:S(2)}) collective-permute-start(s16[400,1024]{1,0:T(8,128)(2,1)S(1)} %stage0.11.refs_1_), channel_id=1, source_target_pairs={{0,4},{4,0},{8,12},{12,8},{16,20},{20,16},{24,28},{28,24},{1,5},{5... | collective-permute-start | bytes 2457608 | tf_op jit(solution)/shard_map/ppermute | solution.py:265
  169.3 26.6 %collective-permute-start.13 = (s16[400,512]{1,0:T(8,128)(2,1)S(1)}, s16[400,512]{1,0:T(8,128)(2,1)S(1)}, u32[]{:S(2)}, u32[]{:S(2)}) collective-permute-start(s16[400,512]{1,0:T(8,128)(2,1)S(1)} %stage1.10.refs_2_), channel_id=1, source_target_pairs={{0,8},{4,12},{8,0},{12,4},{16,24},{20,28},{24,16},{28,20},{1,9},{5... | collective-permute-start | bytes 1228808 | tf_op jit(solution)/shard_map/ppermute | solution.py:265
  189.8 17.2 %collective-permute-start.12 = (s16[400,512]{1,0:T(8,128)(2,1)S(1)}, s16[400,512]{1,0:T(8,128)(2,1)S(1)}, u32[]{:S(2)}, u32[]{:S(2)}) collective-permute-start(s16[400,512]{1,0:T(8,128)(2,1)S(1)} %stage2.9.refs_5_), channel_id=1, source_target_pairs={{0,16},{4,20},{8,24},{12,28},{16,0},{20,4},{24,8},{28,12},{1,17},{... | collective-permute-start | bytes 1228808 | tf_op jit(solution)/shard_map/ppermute | solution.py:265
  195.9 14.3 %collective-permute-start.16 = (s16[400,512]{1,0:T(8,128)(2,1)S(1)}, s16[400,512]{1,0:T(8,128)(2,1)S(1)}, u32[]{:S(2)}, u32[]{:S(2)}) collective-permute-start(s16[400,512]{1,0:T(8,128)(2,1)S(1)} %stage1.11.refs_2_), channel_id=1, source_target_pairs={{0,8},{4,12},{8,0},{12,4},{16,24},{20,28},{24,16},{28,20},{1,9},{5... | collective-permute-start | bytes 1228808 | tf_op jit(solution)/shard_map/ppermute | solution.py:265
  198.2 15.5 %collective-permute-start.15 = (s16[400,256]{1,0:T(8,128)(2,1)S(1)}, s16[400,256]{1,0:T(8,128)(2,1)S(1)}, u32[]{:S(2)}, u32[]{:S(2)}) collective-permute-start(s16[400,256]{1,0:T(8,128)(2,1)S(1)} %stage2.10.refs_5_), channel_id=1, source_target_pairs={{0,16},{4,20},{8,24},{12,28},{16,0},{20,4},{24,8},{28,12},{1,17},{... | collective-permute-start | bytes 614408 | tf_op jit(solution)/shard_map/ppermute | solution.py:265
  212.4 8.5 %collective-permute-start.17 = (s16[400,256]{1,0:T(8,128)(2,1)S(1)}, s16[400,256]{1,0:T(8,128)(2,1)S(1)}, u32[]{:S(2)}, u32[]{:S(2)}) collective-permute-start(s16[400,256]{1,0:T(8,128)(2,1)S(1)} %stage2.11.refs_5_), channel_id=1, source_target_pairs={{0,16},{4,20},{8,24},{12,28},{16,0},{20,4},{24,8},{28,12},{1,17},{... | collective-permute-start | bytes 614408 | tf_op jit(solution)/shard_map/ppermute | solution.py:265
  220.9 2.6 %copy-start.10 = (pred[128]{0:T(512)(128)(4,1)S(1)}, pred[128]{0:T(512)(128)(4,1)}, u32[]{:S(2)}) copy-start(pred[128]{0:T(512)(128)(4,1)} %get-tuple-element.31) | copy-start | bytes 388
  220.9 2.6 %copy-start.11 = (pred[128]{0:T(512)(128)(4,1)S(1)}, pred[128]{0:T(512)(128)(4,1)}, u32[]{:S(2)}) copy-start(pred[128]{0:T(512)(128)(4,1)} %get-tuple-element.32) | copy-start | bytes 388
  (8 other events, 18.2 us)

commit v2 on v1

--- a/solution.py
+++ b/solution.py
@@ -9,7 +9,7 @@
 
 E = 256
 LANES = 128
-CODE_ROWS = 16
+CODE_ROWS = 8
 STEPS = 256.0
 TOP = 32700.0
 TINY = 2.0 ** -100
@@ -150,7 +150,7 @@
         out_ref[:, target : target + width] = as_float(whole_ref[owner, :, column : column + width]) * unit
 
 
-def place(group, n_dp, whole, out, features):
+def place(group, n_dp, whole, out, features, earlier):
     first = min(chunk.first for chunk in group)
     span = sum(chunk.size for chunk in group)
     blocks, column = [], 0
@@ -162,8 +162,9 @@
                 slot = 2 * slot + ((owner >> bit) & 1)
             blocks.append((owner, column, width, lane, chunk.first - first + slot * width))
         column += width
-    operands, in_specs = [whole], [pl.BlockSpec(whole.shape, lambda i: (0, 0, 0))]
-    if out is not None:
+    operands = [whole, earlier]
+    in_specs = [pl.BlockSpec(whole.shape, lambda i: (0, 0, 0)), pl.BlockSpec(memory_space=pl.ANY)]
+    if out is not None and out is not earlier:
         operands.append(out)
         in_specs.append(pl.BlockSpec(memory_space=pl.ANY))
     return pl.pallas_call(
@@ -172,13 +173,13 @@
         in_specs=in_specs,
         out_specs=pl.BlockSpec((whole.shape[1], span), lambda i: (0, first // span)),
         out_shape=jax.ShapeDtypeStruct((whole.shape[1], features), jnp.float32),
-        input_output_aliases={} if out is None else {1: 0},
+        input_output_aliases={} if out is None else {len(operands) - 1: 0},
         compiler_params=pltpu.CompilerParams(vmem_limit_bytes=40 * 1024 * 1024),
         name="place",
     )(*operands)
 
 
-def collect(group, credits, n_dp):
+def collect(credits, n_dp):
     lane = lax.broadcasted_iota(jnp.int32, (E, LANES), 1)
     codes = credits[0][1]
     for k in range(1, len(credits)):
@@ -206,11 +207,14 @@
     return sizes, groups, sequence
 
 
-A, B, C = (0, 1, 2), (1, 0, 2), (1, 2, 0)
-SIZES = [(2, A), (2, A), (4, A), (4, A), (2, A), (2, A)]
-GROUPS = [[0, 1, 2, 3, 4, 5]]
-SEQUENCE = None
-COST = 9_000_000_000
+A, B, C, D = (0, 1, 2), (1, 0, 2), (1, 2, 0), (0, 2, 1)
+SIZES = [(4, A), (4, C), (4, A), (2, D), (2, A)]
+GROUPS = [[0, 1, 2, 3, 4]]
+SEQUENCE = [
+    (0, 0), (1, 0), (2, 0), (0, 1), (1, 1), (3, 0), (2, 1), (0, 2), (4, 0), (1, 2),
+    (3, 1), (4, 1), (2, 2), (0, 3), (1, 3), (3, 2), (4, 2), (2, 3), (3, 3), (4, 3),
+]
+COSTS = [9224000000]
 
 
 def route_table(routes):
@@ -228,15 +232,17 @@
 def gather_rows(residual, cotangent, route_experts, route_buckets, n_dp):
     mine, width = residual.shape
     depth = width // n_dp
+    n_feat, core = lax.axis_size("feat"), lax.axis_index("feat") & 1
     routes = jnp.concatenate([route_experts, route_buckets], 1).astype(jnp.bfloat16)
-    extra = -(-routes.size // (8 * depth)) * 8
-    flat = jnp.pad(routes.reshape(-1), (0, extra * depth - routes.size)).reshape(extra, 1, depth)
-    flat = jnp.broadcast_to(flat, (extra, n_dp, depth)).reshape(extra, width)
-    got = lax.all_to_all(
-        jnp.concatenate([residual, cotangent, flat], 0), "dp", split_axis=1, concat_axis=0, tiled=True
-    ).reshape(n_dp, 2 * mine + extra, depth)
-    rows = got[:, : 2 * mine].reshape(n_dp, 2, mine, depth).transpose(1, 0, 2, 3).reshape(2, n_dp * mine, depth)
-    routes = got[:, 2 * mine :].reshape(n_dp, -1)[:, : routes.size].reshape(n_dp * mine, -1)
+    n_route = routes.shape[1]
+    extra = jnp.broadcast_to(jnp.pad(routes, ((0, 0), (0, LANES - n_route)))[:, None, :], (mine, n_dp, LANES))
+    own = jnp.where(core == 0, residual, cotangent).reshape(mine, n_dp, depth)
+    own = jnp.concatenate([own, extra], 2).transpose(1, 0, 2)
+    got = lax.all_to_all(own, "dp", split_axis=0, concat_axis=0, tiled=True)
+    got = got.reshape(n_dp * mine, depth + LANES)
+    first, routes = got[:, :depth], got[:, depth : depth + n_route]
+    second = lax.ppermute(first, "feat", [(i, i ^ 1) for i in range(n_feat)])
+    rows = jnp.where(core == 0, jnp.stack([first, second]), jnp.stack([second, first]))
     return rows, routes
 
 
@@ -256,10 +262,14 @@
         chunks.append(Chunk(first, units * unit, order))
         first += units * unit
 
-    earlier, credits, out = None, {}, None
-    for n, (c, stage) in enumerate(sequence):
+    earlier, credits, sent, out = None, {}, {}, None
+    for n, (c, stage) in enumerate(sequence + [(-1, g) for g in range(len(groups)) if (-1, g) not in sequence]):
+        if c < 0:
+            group = [chunks[k] for k in groups[stage]]
+            out = earlier = place(group, n_dp, sent[stage], out, features, earlier)
+            continue
         chunk = chunks[c]
-        result = run_stage(chunk, stage, bits, rows, enc, dec, bias, routing, earlier, COST if n != 1 else 1)
+        result = run_stage(chunk, stage, bits, rows, enc, dec, bias, routing, earlier, COSTS[min(n, len(COSTS) - 1)])
         if stage < n_bits:
             partner = [(i, i ^ (1 << chunk.order[stage])) for i in range(n_dp)]
             chunk.messages.append(lax.ppermute(result, "dp", partner))
@@ -267,10 +277,9 @@
         else:
             credits[c] = result
             earlier = result[1]
-            for group in groups:
+            for g, group in enumerate(groups):
                 if c in group and all(k in credits for k in group):
-                    whole = collect([chunks[k] for k in group], [credits[k] for k in group], n_dp)
-                    out = place([chunks[k] for k in group], n_dp, whole, out, features)
+                    sent[g] = collect([credits[k] for k in group], n_dp)
     return out
 
 

time: 254 us -> 211 us (0.83)
  waiting for transfers between devices: 112 us -> 84.5 us
  Pallas kernels: 78.8 us -> 71.7 us
  local copies, waits for them, and re-layouts: 5.48 us -> 0.39 us
  starting transfers between devices: 25.5 us -> 21.3 us
  other arithmetic: 3.2 us -> 5.85 us
    ppermute x18 -> x15, waiting for transfers between devices: 92.4 us -> 73.7 us  [on_device(): chunk.messages.append(lax.ppermute(result, 'dp', partner))]
    all_to_all x1, waiting for transfers between devices: 19.4 us -> 10.5 us  [gather_rows(): got = lax.all_to_all(own, 'dp', split_axis=0, concat_axis=0, tiled=True)]
    pallas_call x24 -> x20, Pallas kernels: 77.1 us -> 70.1 us  [run_stage(): pl.pallas_call(functools.partial(body, tokens, len(chunk.messages)), grid...]
    ppermute x18 -> x15, starting transfers between devices: 18.2 us -> 13.9 us  [on_device(): chunk.messages.append(lax.ppermute(result, 'dp', partner))]
    unnamed x36 -> x16, local copies, waits for them, and re-layouts: 3.94 us -> 0.19 us
  transfers between devices with their start and end apart: 19 -> 17, of which waited for: 9 -> 10; matrix products, arithmetic and copies ran while one was open for 1% -> 1% of each run, Pallas kernels for 26% -> 29%
where the time goes in v2:
time: 211 us; the launch traced here: 210 us
  waiting for transfers between devices  84.5 us (40%)
  Pallas kernels  71.7 us (34%)
  blocking collectives  26.2 us (12%)
  starting transfers between devices  21.3 us (10%)
  other arithmetic  5.85 us (3%)
    ppermute x15, waiting for transfers between devices, on_device(): chunk.messages.append(lax.ppermute(result, 'dp', partner))  73.7 us
    pallas_call x20, Pallas kernels, run_stage(): pl.pallas_call(functools.partial(body, tokens, len(chunk.messages)), grid...  70.1 us
    all_to_all x1, blocking collectives, collect(): whole = lax.all_to_all(whole, 'dp', split_axis=0, concat_axis=0, tiled=True)  26.2 us
    ppermute x15, starting transfers between devices, on_device(): chunk.messages.append(lax.ppermute(result, 'dp', partner))  13.9 us
    all_to_all x1, waiting for transfers between devices, gather_rows(): got = lax.all_to_all(own, 'dp', split_axis=0, concat_axis=0, tiled=True)  10.5 us
    all_to_all x1, starting transfers between devices, gather_rows(): got = lax.all_to_all(own, 'dp', split_axis=0, concat_axis=0, tiled=True)  7.25 us
  transfers between devices with their start and end apart: 17, of which 10 were waited for; matrix products, arithmetic and copies ran while one was open for 1% of the time, Pallas kernels for 29%

profile of v2, /device:TPU:0, one launch (start us, length us, event | category | flops | bytes accessed | tf_op | source)
XLA Modules:
  0.0 210.4 jit_solution(10052794724777478914)
XLA Ops:
  3.4 7.3 %all-to-all-start = ((bf16[8,24,1024]{2,1,0:T(8,128)(2,1)}), bf16[8,24,1024]{2,1,0:T(8,128)(2,1)S(1)}, u32[]{:S(2)}, u32[]{:S(2)}) async-start(bf16[8,24,1024]{2,1,0:T(8,128)(2,1)} %maximum_bitcast_fusion), calls=%async_computation | async-start | bytes 786432 | tf_op jit(solution)/shard_map/all_to_all | solution.py:241
  11.8 10.5 %all-to-all-done = bf16[8,24,1024]{2,1,0:T(8,128)(2,1)S(1)} async-done(((bf16[8,24,1024]{2,1,0:T(8,128)(2,1)}), bf16[8,24,1024]{2,1,0:T(8,128)(2,1)S(1)}, u32[]{:S(2)}, u32[]{:S(2)}) %all-to-all-start) | async-done | bytes 393248 | tf_op jit(solution)/shard_map/all_to_all | solution.py:241
  24.3 6.1 %stage0.5.refs_0_ = s16[392,2048]{1,0:T(8,128)(2,1)S(1)} custom-call(s32[3]{0:T(128)S(1)} %shift-right-arithmetic_and_fusion.where_ref, bf16[2,192,896]{2,1,0:T(8,128)(2,1)S(1)} %maximum_select_fusion.rows_ref, bf16[896,16384]{1,0:T(8,128)(2,1)} %enc_ref.39, bf16[16384,896]{1,0:T(8,128)(2,1)} %dec_ref.39), custom_call_target="tpu_custom_call" | custom-call | flops 9223999488 | bytes 1 | tf_op jit(solution)/shard_map/stage0/pallas_call | solution.py:133
  31.9 6.1 %stage0.6.refs_0_ = s16[392,2048]{1,0:T(8,128)(2,1)S(1)} custom-call(s32[3]{0:T(128)S(1)} %shift-right-arithmetic_and_fusion.where_ref, bf16[2,192,896]{2,1,0:T(8,128)(2,1)S(1)} %maximum_select_fusion.rows_ref, bf16[896,16384]{1,0:T(8,128)(2,1)} %enc_ref.39, bf16[16384,896]{1,0:T(8,128)(2,1)} %dec_ref.39, s16[392,2048]{1,0:T(8,128)(2,1)S(1)} %stage0.5.refs_0_), custom_call_target="tpu_custom_call" | custom-call | flops 9223999488 | bytes 1 | tf_op jit(solution)/shard_map/stage0/pallas_call | solution.py:133
  38.1 6.1 %stage0.7.refs_1_ = s16[392,2048]{1,0:T(8,128)(2,1)S(1)} custom-call(s32[3]{0:T(128)S(1)} %shift-right-arithmetic_and_fusion.where_ref, bf16[2,192,896]{2,1,0:T(8,128)(2,1)S(1)} %maximum_select_fusion.rows_ref, bf16[896,16384]{1,0:T(8,128)(2,1)} %enc_ref.39, bf16[16384,896]{1,0:T(8,128)(2,1)} %dec_ref.39, s16[392,2048]{1,0:T(8,128)(2,1)S(1)} %stage0.6.refs_0_), custom_call_target="tpu_custom_call" | custom-call | flops 9223999488 | bytes 1 | tf_op jit(solution)/shard_map/stage0/pallas_call | solution.py:133
  45.8 22.6 %collective-permute-done.1.refs_0_ = s16[392,2048]{1,0:T(8,128)(2,1)S(1)} collective-permute-done((s16[392,2048]{1,0:T(8,128)(2,1)S(1)}, s16[392,2048]{1,0:T(8,128)(2,1)S(1)}, u32[]{:S(2)}, u32[]{:S(2)}) %collective-permute-start.1) | collective-permute-done | bytes 1605664 | tf_op jit(solution)/shard_map/ppermute | solution.py:275
  68.4 3.7 %stage1.5.refs_1_ = s16[392,1024]{1,0:T(8,128)(2,1)S(1)} custom-call(s32[3]{0:T(128)S(1)} %shift-right-arithmetic_and_fusion.where_ref, bf16[2,192,896]{2,1,0:T(8,128)(2,1)S(1)} %maximum_select_fusion.rows_ref, bf16[896,16384]{1,0:T(8,128)(2,1)} %enc_ref.39, bf16[16384,896]{1,0:T(8,128)(2,1)} %dec_ref.39, ...), custom_call_target="tpu_custom_call" | custom-call | flops 9223999488 | bytes 1 | tf_op jit(solution)/shard_map/stage1/pallas_call | solution.py:133
  73.2 2.9 %collective-permute-done.4.refs_0_ = s16[392,2048]{1,0:T(8,128)(2,1)S(1)} collective-permute-done((s16[392,2048]{1,0:T(8,128)(2,1)S(1)}, s16[392,2048]{1,0:T(8,128)(2,1)S(1)}, u32[]{:S(2)}, u32[]{:S(2)}) %collective-permute-start.4) | collective-permute-done | bytes 1605664 | tf_op jit(solution)/shard_map/ppermute | solution.py:275
  76.1 3.7 %stage1.6.refs_0_ = s16[392,1024]{1,0:T(8,128)(2,1)S(1)} custom-call(s32[3]{0:T(128)S(1)} %shift-right-arithmetic_and_fusion.where_ref, bf16[2,192,896]{2,1,0:T(8,128)(2,1)S(1)} %maximum_select_fusion.rows_ref, bf16[896,16384]{1,0:T(8,128)(2,1)} %enc_ref.39, bf16[16384,896]{1,0:T(8,128)(2,1)} %dec_ref.39, ...), custom_call_target="tpu_custom_call" | custom-call | flops 9223999488 | bytes 1 | tf_op jit(solution)/shard_map/stage1/pallas_call | solution.py:133
  79.9 3.7 %stage0.8.refs_1_ = s16[392,1024]{1,0:T(8,128)(2,1)S(1)} custom-call(s32[3]{0:T(128)S(1)} %shift-right-arithmetic_and_fusion.where_ref, bf16[2,192,896]{2,1,0:T(8,128)(2,1)S(1)} %maximum_select_fusion.rows_ref, bf16[896,16384]{1,0:T(8,128)(2,1)} %enc_ref.39, bf16[16384,896]{1,0:T(8,128)(2,1)} %dec_ref.39, s16[392,1024]{1,0:T(8,128)(2,1)S(1)} %stage1.6.refs_0_), custom_call_target="tpu_custom_call" | custom-call | flops 9223999488 | bytes 1 | tf_op jit(solution)/shard_map/stage0/pallas_call | solution.py:133
  85.1 17.8 %collective-permute-done.3.refs_0_ = s16[392,2048]{1,0:T(8,128)(2,1)S(1)} collective-permute-done((s16[392,2048]{1,0:T(8,128)(2,1)S(1)}, s16[392,2048]{1,0:T(8,128)(2,1)S(1)}, u32[]{:S(2)}, u32[]{:S(2)}) %collective-permute-start.3) | collective-permute-done | bytes 1605664 | tf_op jit(solution)/shard_map/ppermute | solution.py:275
  102.8 3.7 %stage1.7.refs_2_ = s16[392,1024]{1,0:T(8,128)(2,1)S(1)} custom-call(s32[3]{0:T(128)S(1)} %shift-right-arithmetic_and_fusion.where_ref, bf16[2,192,896]{2,1,0:T(8,128)(2,1)S(1)} %maximum_select_fusion.rows_ref, bf16[896,16384]{1,0:T(8,128)(2,1)} %enc_ref.39, bf16[16384,896]{1,0:T(8,128)(2,1)} %dec_ref.39, ...), custom_call_target="tpu_custom_call" | custom-call | flops 9223999488 | bytes 1 | tf_op jit(solution)/shard_map/stage1/pallas_call | solution.py:133
  107.6 2.8 %stage2.5.refs_0_ = s16[392,512]{1,0:T(8,128)(2,1)S(1)} custom-call(s32[3]{0:T(128)S(1)} %shift-right-arithmetic_and_fusion.where_ref, bf16[2,192,896]{2,1,0:T(8,128)(2,1)S(1)} %maximum_select_fusion.rows_ref, bf16[896,16384]{1,0:T(8,128)(2,1)} %enc_ref.39, bf16[16384,896]{1,0:T(8,128)(2,1)} %dec_ref.39, ...), custom_call_target="tpu_custom_call" | custom-call | flops 9223999488 | bytes 1 | tf_op jit(solution)/shard_map/stage2/pallas_call | solution.py:133
  111.2 3.9 %stage0.9.refs_2_ = s16[392,1024]{1,0:T(8,128)(2,1)S(1)} custom-call(s32[3]{0:T(128)S(1)} %shift-right-arithmetic_and_fusion.where_ref, bf16[2,192,896]{2,1,0:T(8,128)(2,1)S(1)} %maximum_select_fusion.rows_ref, bf16[896,16384]{1,0:T(8,128)(2,1)} %enc_ref.39, bf16[16384,896]{1,0:T(8,128)(2,1)} %dec_ref.39, s16[392,512]{1,0:T(8,128)(2,1)S(1)} %stage2.5.refs_0_), custom_call_target="tpu_custom_call" | custom-call | flops 9223999488 | bytes 1 | tf_op jit(solution)/shard_map/stage0/pallas_call | solution.py:133
  118.9 2.8 %stage2.6.refs_1_ = s16[392,512]{1,0:T(8,128)(2,1)S(1)} custom-call(s32[3]{0:T(128)S(1)} %shift-right-arithmetic_and_fusion.where_ref, bf16[2,192,896]{2,1,0:T(8,128)(2,1)S(1)} %maximum_select_fusion.rows_ref, bf16[896,16384]{1,0:T(8,128)(2,1)} %enc_ref.39, bf16[16384,896]{1,0:T(8,128)(2,1)} %dec_ref.39, ...), custom_call_target="tpu_custom_call" | custom-call | flops 9223999488 | bytes 1 | tf_op jit(solution)/shard_map/stage2/pallas_call | solution.py:133
  125.0 12.2 %collective-permute-done.7.refs_0_ = s16[392,1024]{1,0:T(8,128)(2,1)S(1)} collective-permute-done((s16[392,1024]{1,0:T(8,128)(2,1)S(1)}, s16[392,1024]{1,0:T(8,128)(2,1)S(1)}, u32[]{:S(2)}, u32[]{:S(2)}) %collective-permute-start.7) | collective-permute-done | bytes 802848 | tf_op jit(solution)/shard_map/ppermute | solution.py:275
  142.0 2.8 %stage2.7.refs_5_ = s16[392,512]{1,0:T(8,128)(2,1)S(1)} custom-call(s32[3]{0:T(128)S(1)} %shift-right-arithmetic_and_fusion.where_ref, bf16[2,192,896]{2,1,0:T(8,128)(2,1)S(1)} %maximum_select_fusion.rows_ref, bf16[896,16384]{1,0:T(8,128)(2,1)} %enc_ref.39, bf16[16384,896]{1,0:T(8,128)(2,1)} %dec_ref.39, ...), custom_call_target="tpu_custom_call" | custom-call | flops 9223999488 | bytes 1 | tf_op jit(solution)/shard_map/stage2/pallas_call | solution.py:133
  144.9 3.2 %credit.5 = (s16[256,512]{1,0:T(8,128)(2,1)S(1)}, s16[256,128]{1,0:T(8,128)(2,1)S(1)}) custom-call(s32[3]{0:T(128)S(1)} %shift-right-arithmetic_and_fusion.where_ref, bf16[2,192,896]{2,1,0:T(8,128)(2,1)S(1)} %maximum_select_fusion.rows_ref, bf16[896,16384]{1,0:T(8,128)(2,1)} %enc_ref.39, bf16[16384,896]{1,0:T(8,128)(2,1)} %dec_ref.39, ...), custom_call_target="tpu_custom_call" | custom-call | flops 9223999488 | bytes 1 | tf_op jit(solution)/shard_map/credit/pallas_call | solution.py:133
  148.2 3.2 %credit.6 = (s16[256,512]{1,0:T(8,128)(2,1)S(1)}, s16[256,128]{1,0:T(8,128)(2,1)S(1)}) custom-call(s32[3]{0:T(128)S(1)} %shift-right-arithmetic_and_fusion.where_ref, bf16[2,192,896]{2,1,0:T(8,128)(2,1)S(1)} %maximum_select_fusion.rows_ref, bf16[896,16384]{1,0:T(8,128)(2,1)} %enc_ref.39, bf16[16384,896]{1,0:T(8,128)(2,1)} %dec_ref.39, ...), custom_call_target="tpu_custom_call" | custom-call | flops 9223999488 | bytes 1 | tf_op jit(solution)/shard_map/credit/pallas_call | solution.py:133
  151.4 8.3 %collective-permute-done.13.refs_1_ = s16[392,512]{1,0:T(8,128)(2,1)S(1)} collective-permute-done((s16[392,512]{1,0:T(8,128)(2,1)S(1)}, s16[392,512]{1,0:T(8,128)(2,1)S(1)}, u32[]{:S(2)}, u32[]{:S(2)}) %collective-permute-start.13) | collective-permute-done | bytes 401440 | tf_op jit(solution)/shard_map/ppermute | solution.py:275
  164.3 2.9 %collective-permute-start.15 = (s16[392,256]{1,0:T(8,128)(2,1)S(1)}, s16[392,256]{1,0:T(8,128)(2,1)S(1)}, u32[]{:S(2)}, u32[]{:S(2)}) collective-permute-start(s16[392,256]{1,0:T(8,128)(2,1)S(1)} %stage2.9.refs_5_), channel_id=1, source_target_pairs={{0,16},{4,20},{8,24},{12,28},{16,0},{20,4},{24,8},{28,12},{1,17},{... | collective-permute-start | bytes 602120 | tf_op jit(solution)/shard_map/ppermute | solution.py:275
  167.2 6.8 %collective-permute-done.11.refs_2_ = s16[392,512]{1,0:T(8,128)(2,1)S(1)} collective-permute-done((s16[392,512]{1,0:T(8,128)(2,1)S(1)}, s16[392,512]{1,0:T(8,128)(2,1)S(1)}, u32[]{:S(2)}, u32[]{:S(2)}) %collective-permute-start.11) | collective-permute-done | bytes 401440 | tf_op jit(solution)/shard_map/ppermute | solution.py:275
  173.9 3.2 %credit.7 = (s16[256,512]{1,0:T(8,128)(2,1)S(1)}, s16[256,128]{1,0:T(8,128)(2,1)S(1)}) custom-call(s32[3]{0:T(128)S(1)} %shift-right-arithmetic_and_fusion.where_ref, bf16[2,192,896]{2,1,0:T(8,128)(2,1)S(1)} %maximum_select_fusion.rows_ref, bf16[896,16384]{1,0:T(8,128)(2,1)} %enc_ref.39, bf16[16384,896]{1,0:T(8,128)(2,1)} %dec_ref.39, ...), custom_call_target="tpu_custom_call" | custom-call | flops 9223999488 | bytes 1 | tf_op jit(solution)/shard_map/credit/pallas_call | solution.py:133
  182.5 26.2 %all_to_all.14.whole_ref = s16[8,32,2176]{2,1,0:T(8,128)(2,1)S(1)} all-to-all(s16[8,32,2176]{2,1,0:T(8,128)(2,1)S(1)} %bitcast.26), channel_id=1, replica_groups=mesh['dp'=8,'feat'=4] {'dp'}, dimensions={0} | all-to-all | bytes 2228224 | tf_op jit(solution)/shard_map/all_to_all | solution.py:188
  (66 shorter events, 37.4 us)
Async XLA Ops:
  3.4 18.9 %all-to-all-start = ((bf16[8,24,1024]{2,1,0:T(8,128)(2,1)}), bf16[8,24,1024]{2,1,0:T(8,128)(2,1)S(1)}, u32[]{:S(2)}, u32[]{:S(2)}) async-start(bf16[8,24,1024]{2,1,0:T(8,128)(2,1)} %maximum_bitcast_fusion), calls=%async_computation | async-start | bytes 786432 | tf_op jit(solution)/shard_map/all_to_all | solution.py:241
  22.5 1.7 collective-permute-start
  30.4 38.0 %collective-permute-start.1 = (s16[392,2048]{1,0:T(8,128)(2,1)S(1)}, s16[392,2048]{1,0:T(8,128)(2,1)S(1)}, u32[]{:S(2)}, u32[]{:S(2)}) collective-permute-start(s16[392,2048]{1,0:T(8,128)(2,1)S(1)} %stage0.5.refs_0_), channel_id=1, source_target_pairs={{0,4},{4,0},{8,12},{12,8},{16,20},{20,16},{24,28},{28,24},{1,5},{5... | collective-permute-start | bytes 4816904 | tf_op jit(solution)/shard_map/ppermute | solution.py:275
  38.0 38.0 %collective-permute-start.4 = (s16[392,2048]{1,0:T(8,128)(2,1)S(1)}, s16[392,2048]{1,0:T(8,128)(2,1)S(1)}, u32[]{:S(2)}, u32[]{:S(2)}) collective-permute-start(s16[392,2048]{1,0:T(8,128)(2,1)S(1)} %stage0.6.refs_0_), channel_id=1, source_target_pairs={{0,8},{4,12},{8,0},{12,4},{16,24},{20,28},{24,16},{28,20},{1,9},{5... | collective-permute-start | bytes 4816904 | tf_op jit(solution)/shard_map/ppermute | solution.py:275
  44.2 58.6 %collective-permute-start.3 = (s16[392,2048]{1,0:T(8,128)(2,1)S(1)}, s16[392,2048]{1,0:T(8,128)(2,1)S(1)}, u32[]{:S(2)}, u32[]{:S(2)}) collective-permute-start(s16[392,2048]{1,0:T(8,128)(2,1)S(1)} %stage0.7.refs_1_), channel_id=1, source_target_pairs={{0,4},{4,0},{8,12},{12,8},{16,20},{20,16},{24,28},{28,24},{1,5},{5... | collective-permute-start | bytes 4816904 | tf_op jit(solution)/shard_map/ppermute | solution.py:275
  72.2 35.4 %collective-permute-start.2 = (s16[392,1024]{1,0:T(8,128)(2,1)S(1)}, s16[392,1024]{1,0:T(8,128)(2,1)S(1)}, u32[]{:S(2)}, u32[]{:S(2)}) collective-permute-start(s16[392,1024]{1,0:T(8,128)(2,1)S(1)} %stage1.5.refs_1_), channel_id=1, source_target_pairs={{0,8},{4,12},{8,0},{12,4},{16,24},{20,28},{24,16},{28,20},{1,9},{5... | collective-permute-start | bytes 2408456 | tf_op jit(solution)/shard_map/ppermute | solution.py:275
  79.8 39.1 %collective-permute-start.9 = (s16[392,1024]{1,0:T(8,128)(2,1)S(1)}, s16[392,1024]{1,0:T(8,128)(2,1)S(1)}, u32[]{:S(2)}, u32[]{:S(2)}) collective-permute-start(s16[392,1024]{1,0:T(8,128)(2,1)S(1)} %stage1.6.refs_0_), channel_id=1, source_target_pairs={{0,16},{4,20},{8,24},{12,28},{16,0},{20,4},{24,8},{28,12},{1,17},{... | collective-permute-start | bytes 2408456 | tf_op jit(solution)/shard_map/ppermute | solution.py:275
  83.6 38.4 %collective-permute-start.8 = (s16[392,1024]{1,0:T(8,128)(2,1)S(1)}, s16[392,1024]{1,0:T(8,128)(2,1)S(1)}, u32[]{:S(2)}, u32[]{:S(2)}) collective-permute-start(s16[392,1024]{1,0:T(8,128)(2,1)S(1)} %stage0.8.refs_1_), channel_id=1, source_target_pairs={{0,4},{4,0},{8,12},{12,8},{16,20},{20,16},{24,28},{28,24},{1,5},{5... | collective-permute-start | bytes 2408456 | tf_op jit(solution)/shard_map/ppermute | solution.py:275
  106.6 35.4 %collective-permute-start.6 = (s16[392,1024]{1,0:T(8,128)(2,1)S(1)}, s16[392,1024]{1,0:T(8,128)(2,1)S(1)}, u32[]{:S(2)}, u32[]{:S(2)}) collective-permute-start(s16[392,1024]{1,0:T(8,128)(2,1)S(1)} %stage1.7.refs_2_), channel_id=1, source_target_pairs={{0,8},{4,12},{8,0},{12,4},{16,24},{20,28},{24,16},{28,20},{1,9},{5... | collective-permute-start | bytes 2408456 | tf_op jit(solution)/shard_map/ppermute | solution.py:275
  110.4 34.6 %collective-permute-start.5 = (s16[392,512]{1,0:T(8,128)(2,1)S(1)}, s16[392,512]{1,0:T(8,128)(2,1)S(1)}, u32[]{:S(2)}, u32[]{:S(2)}) collective-permute-start(s16[392,512]{1,0:T(8,128)(2,1)S(1)} %stage2.5.refs_0_), channel_id=1, source_target_pairs={{0,16},{4,20},{8,24},{12,28},{16,0},{20,4},{24,8},{28,12},{1,17},{... | collective-permute-start | bytes 1204232 | tf_op jit(solution)/shard_map/ppermute | solution.py:275
  115.1 22.1 %collective-permute-start.7 = (s16[392,1024]{1,0:T(8,128)(2,1)S(1)}, s16[392,1024]{1,0:T(8,128)(2,1)S(1)}, u32[]{:S(2)}, u32[]{:S(2)}) collective-permute-start(s16[392,1024]{1,0:T(8,128)(2,1)S(1)} %stage0.9.refs_2_), channel_id=1, source_target_pairs={{0,4},{4,0},{8,12},{12,8},{16,20},{20,16},{24,28},{28,24},{1,5},{5... | collective-permute-start | bytes 2408456 | tf_op jit(solution)/shard_map/ppermute | solution.py:275
  121.7 26.4 %collective-permute-start.10 = (s16[392,512]{1,0:T(8,128)(2,1)S(1)}, s16[392,512]{1,0:T(8,128)(2,1)S(1)}, u32[]{:S(2)}, u32[]{:S(2)}) collective-permute-start(s16[392,512]{1,0:T(8,128)(2,1)S(1)} %stage2.6.refs_1_), channel_id=1, source_target_pairs={{0,4},{4,0},{8,12},{12,8},{16,20},{20,16},{24,28},{28,24},{1,5},{5... | collective-permute-start | bytes 1204232 | tf_op jit(solution)/shard_map/ppermute | solution.py:275
  124.7 35.0 %collective-permute-start.13 = (s16[392,512]{1,0:T(8,128)(2,1)S(1)}, s16[392,512]{1,0:T(8,128)(2,1)S(1)}, u32[]{:S(2)}, u32[]{:S(2)}) collective-permute-start(s16[392,512]{1,0:T(8,128)(2,1)S(1)} %stage1.8.refs_1_), channel_id=1, source_target_pairs={{0,16},{4,20},{8,24},{12,28},{16,0},{20,4},{24,8},{28,12},{1,17},{... | collective-permute-start | bytes 1204232 | tf_op jit(solution)/shard_map/ppermute | solution.py:275
  140.0 4.9 %copy-start = (f32[16384]{0:T(1024)S(1)}, f32[16384]{0:T(1024)}, u32[]{:S(2)}) copy-start(f32[16384]{0:T(1024)} %param.10) | copy-start | bytes 196612
  140.0 22.0 %collective-permute-start.12 = (s16[392,512]{1,0:T(8,128)(2,1)S(1)}, s16[392,512]{1,0:T(8,128)(2,1)S(1)}, u32[]{:S(2)}, u32[]{:S(2)}) collective-permute-start(s16[392,512]{1,0:T(8,128)(2,1)S(1)} %stage1.9.refs_2_), channel_id=1, source_target_pairs={{0,8},{4,12},{8,0},{12,4},{16,24},{20,28},{24,16},{28,20},{1,9},{5... | collective-permute-start | bytes 1204232 | tf_op jit(solution)/shard_map/ppermute | solution.py:275
  144.8 29.1 %collective-permute-start.11 = (s16[392,512]{1,0:T(8,128)(2,1)S(1)}, s16[392,512]{1,0:T(8,128)(2,1)S(1)}, u32[]{:S(2)}, u32[]{:S(2)}) collective-permute-start(s16[392,512]{1,0:T(8,128)(2,1)S(1)} %stage2.7.refs_5_), channel_id=1, source_target_pairs={{0,16},{4,20},{8,24},{12,28},{16,0},{20,4},{24,8},{28,12},{1,17},{... | collective-permute-start | bytes 1204232 | tf_op jit(solution)/shard_map/ppermute | solution.py:275
  161.9 15.2 %collective-permute-start.14 = (s16[392,256]{1,0:T(8,128)(2,1)S(1)}, s16[392,256]{1,0:T(8,128)(2,1)S(1)}, u32[]{:S(2)}, u32[]{:S(2)}) collective-permute-start(s16[392,256]{1,0:T(8,128)(2,1)S(1)} %stage2.8.refs_2_), channel_id=1, source_target_pairs={{0,8},{4,12},{8,0},{12,4},{16,24},{20,28},{24,16},{28,20},{1,9},{5... | collective-permute-start | bytes 602120 | tf_op jit(solution)/shard_map/ppermute | solution.py:275
  164.3 15.5 %collective-permute-start.15 = (s16[392,256]{1,0:T(8,128)(2,1)S(1)}, s16[392,256]{1,0:T(8,128)(2,1)S(1)}, u32[]{:S(2)}, u32[]{:S(2)}) collective-permute-start(s16[392,256]{1,0:T(8,128)(2,1)S(1)} %stage2.9.refs_5_), channel_id=1, source_target_pairs={{0,16},{4,20},{8,24},{12,28},{16,0},{20,4},{24,8},{28,12},{1,17},{... | collective-permute-start | bytes 602120 | tf_op jit(solution)/shard_map/ppermute | solution.py:275
  179.8 2.6 %copy-start.1 = (pred[128]{0:T(512)(128)(4,1)S(1)}, pred[128]{0:T(512)(128)(4,1)}, u32[]{:S(2)}) copy-start(pred[128]{0:T(512)(128)(4,1)} %get-tuple-element.27) | copy-start | bytes 388
  179.8 2.6 %copy-start.2 = (pred[128]{0:T(512)(128)(4,1)S(1)}, pred[128]{0:T(512)(128)(4,1)}, u32[]{:S(2)}) copy-start(pred[128]{0:T(512)(128)(4,1)} %get-tuple-element.28) | copy-start | bytes 388
  179.8 2.6 %copy-start.3 = (pred[128]{0:T(512)(128)(4,1)S(1)}, pred[128]{0:T(512)(128)(4,1)}, u32[]{:S(2)}) copy-start(pred[128]{0:T(512)(128)(4,1)} %get-tuple-element.29) | copy-start | bytes 388
  179.8 2.6 %copy-start.4 = (pred[128]{0:T(512)(128)(4,1)S(1)}, pred[128]{0:T(512)(128)(4,1)}, u32[]{:S(2)}) copy-start(pred[128]{0:T(512)(128)(4,1)} %get-tuple-element.30) | copy-start | bytes 388

commit v3 on v2

--- a/solution.py
+++ b/solution.py
@@ -105,7 +105,7 @@
         return first // block + i
 
     in_specs = [
-        pl.BlockSpec((2, tokens, depth), lambda i, w: (0, 0, 0)),
+        pl.BlockSpec(memory_space=pltpu.VMEM),
         pl.BlockSpec((depth, block), lambda i, w: (0, at(i, w))),
         pl.BlockSpec((block, depth), lambda i, w: (at(i, w), 0)),
     ]
@@ -115,7 +115,7 @@
         operands.append(message)
     if last:
         in_specs.append(pl.BlockSpec((1, block), lambda i, w: (0, at(i, w))))
-        in_specs.append(pl.BlockSpec(routing.shape, lambda i, w: (0, 0)))
+        in_specs.append(pl.BlockSpec(memory_space=pltpu.VMEM))
         operands += [bias, routing]
         body = credit_kernel
         out_shape = [
@@ -208,13 +208,15 @@
 
 
 A, B, C, D = (0, 1, 2), (1, 0, 2), (1, 2, 0), (0, 2, 1)
-SIZES = [(4, A), (4, C), (4, A), (2, D), (2, A)]
-GROUPS = [[0, 1, 2, 3, 4]]
+SIZES = [(2, A), (2, C), (2, A), (2, A), (2, B), (2, A), (2, A), (1, D), (1, A)]
+GROUPS = [[0, 1, 2, 3], [4, 5, 6, 7, 8]]
 SEQUENCE = [
-    (0, 0), (1, 0), (2, 0), (0, 1), (1, 1), (3, 0), (2, 1), (0, 2), (4, 0), (1, 2),
-    (3, 1), (4, 1), (2, 2), (0, 3), (1, 3), (3, 2), (4, 2), (2, 3), (3, 3), (4, 3),
+    (0, 0), (1, 0), (2, 0), (3, 0), (0, 1), (1, 1), (4, 0), (0, 2), (2, 1), (1, 2),
+    (5, 0), (3, 1), (1, 3), (0, 3), (4, 1), (6, 0), (2, 2), (5, 1), (3, 2), (4, 2),
+    (7, 0), (2, 3), (3, 3), (8, 0), (6, 1), (5, 2), (7, 1), (4, 3), (8, 1), (-1, 0),
+    (6, 2), (7, 2), (8, 2), (5, 3), (7, 3), (6, 3), (8, 3),
 ]
-COSTS = [9224000000]
+COSTS = [2306000000]
 
 
 def route_table(routes):

time: 211 us -> 207 us (0.981)
  waiting for transfers between devices: 84.5 us -> 30.5 us
  Pallas kernels: 71.7 us -> 106 us
  starting transfers between devices: 21.3 us -> 43.1 us
  blocking collectives: 26.2 us -> 15.8 us
  local copies, waits for them, and re-layouts: 0.39 us -> 3.54 us
    ppermute x15 -> x27, waiting for transfers between devices: 73.7 us -> 19 us  [on_device(): chunk.messages.append(lax.ppermute(result, 'dp', partner))]
    pallas_call x20 -> x36, Pallas kernels: 70.1 us -> 102 us  [run_stage(): pl.pallas_call(functools.partial(body, tokens, len(chunk.messages)), grid...]
    ppermute x15 -> x27, starting transfers between devices: 13.9 us -> 31.6 us  [on_device(): chunk.messages.append(lax.ppermute(result, 'dp', partner))]
    all_to_all x1, blocking collectives: 26.2 us -> 15.8 us  [collect(): whole = lax.all_to_all(whole, 'dp', split_axis=0, concat_axis=0, tiled=True)]
    all_to_all x0 -> x1, starting transfers between devices: none -> 4.2 us  [collect(): whole = lax.all_to_all(whole, 'dp', split_axis=0, concat_axis=0, tiled=True)]
    unnamed x16 -> x52, local copies, waits for them, and re-layouts: 0.19 us -> 3.34 us
  transfers between devices with their start and end apart: 17 -> 30, of which waited for: 10 -> 10; matrix products, arithmetic and copies ran while one was open for 1% -> 2% of each run, Pallas kernels for 29% -> 48%
where the time goes in v3:
time: 207 us; the launch traced here: 206 us
  Pallas kernels  106 us (51%)
  starting transfers between devices  43.1 us (21%)
  waiting for transfers between devices  30.5 us (15%)
  blocking collectives  15.8 us (8%)
  other arithmetic  6.4 us (3%)
  local copies, waits for them, and re-layouts  3.54 us (2%)
    pallas_call x36, Pallas kernels, run_stage(): pl.pallas_call(functools.partial(body, tokens, len(chunk.messages)), grid...  102 us
    ppermute x27, starting transfers between devices, on_device(): chunk.messages.append(lax.ppermute(result, 'dp', partner))  31.6 us
    ppermute x27, waiting for transfers between devices, on_device(): chunk.messages.append(lax.ppermute(result, 'dp', partner))  19 us
    all_to_all x1, blocking collectives, collect(): whole = lax.all_to_all(whole, 'dp', split_axis=0, concat_axis=0, tiled=True)  15.8 us
    all_to_all x1, waiting for transfers between devices, gather_rows(): got = lax.all_to_all(own, 'dp', split_axis=0, concat_axis=0, tiled=True)  9.98 us
    all_to_all x1, starting transfers between devices, gather_rows(): got = lax.all_to_all(own, 'dp', split_axis=0, concat_axis=0, tiled=True)  7.25 us
    all_to_all x1, starting transfers between devices, collect(): whole = lax.all_to_all(whole, 'dp', split_axis=0, concat_axis=0, tiled=True)  4.2 us
  transfers between devices with their start and end apart: 30, of which 10 were waited for; matrix products, arithmetic and copies ran while one was open for 2% of the time, Pallas kernels for 48%

profile of v3, /device:TPU:0, one launch (start us, length us, event | category | flops | bytes accessed | tf_op | source)
XLA Modules:
  0.0 205.8 jit_solution(14337311135625394823)
XLA Ops:
  3.4 7.3 %all-to-all-start = ((bf16[8,24,1024]{2,1,0:T(8,128)(2,1)}), bf16[8,24,1024]{2,1,0:T(8,128)(2,1)S(1)}, u32[]{:S(2)}, u32[]{:S(2)}) async-start(bf16[8,24,1024]{2,1,0:T(8,128)(2,1)} %maximum_bitcast_fusion), calls=%async_computation | async-start | bytes 786432 | tf_op jit(solution)/shard_map/all_to_all | solution.py:243
  12.3 10.0 %all-to-all-done = bf16[8,24,1024]{2,1,0:T(8,128)(2,1)S(1)} async-done(((bf16[8,24,1024]{2,1,0:T(8,128)(2,1)}), bf16[8,24,1024]{2,1,0:T(8,128)(2,1)S(1)}, u32[]{:S(2)}, u32[]{:S(2)}) %all-to-all-start) | async-done | bytes 393248 | tf_op jit(solution)/shard_map/all_to_all | solution.py:243
  24.2 3.7 %stage0.9.refs_0_ = s16[392,1024]{1,0:T(8,128)(2,1)S(1)} custom-call(s32[3]{0:T(128)S(1)} %shift-right-arithmetic_and_fusion.where_ref, bf16[2,192,896]{2,1,0:T(8,128)(2,1)S(1)} %maximum_select_fusion.rows_ref, bf16[896,16384]{1,0:T(8,128)(2,1)} %enc_ref.71, bf16[16384,896]{1,0:T(8,128)(2,1)} %dec_ref.71), custom_call_target="tpu_custom_call" | custom-call | flops 2305999872 | bytes 1 | tf_op jit(solution)/shard_map/stage0/pallas_call | solution.py:133
  29.4 4.3 %stage0.10.refs_0_ = s16[392,1024]{1,0:T(8,128)(2,1)} custom-call(s32[3]{0:T(128)S(1)} %shift-right-arithmetic_and_fusion.where_ref, bf16[2,192,896]{2,1,0:T(8,128)(2,1)S(1)} %maximum_select_fusion.rows_ref, bf16[896,16384]{1,0:T(8,128)(2,1)} %enc_ref.71, bf16[16384,896]{1,0:T(8,128)(2,1)} %dec_ref.71, s16[392,1024]{1,0:T(8,128)(2,1)S(1)} %stage0.9.refs_0_), custom_call_target="tpu_custom_call" | custom-call | flops 2305999872 | bytes 1 | tf_op jit(solution)/shard_map/stage0/pallas_call | solution.py:133
  35.0 3.7 %stage0.11.refs_0_ = s16[392,1024]{1,0:T(8,128)(2,1)S(1)} custom-call(s32[3]{0:T(128)S(1)} %shift-right-arithmetic_and_fusion.where_ref, bf16[2,192,896]{2,1,0:T(8,128)(2,1)S(1)} %maximum_select_fusion.rows_ref, bf16[896,16384]{1,0:T(8,128)(2,1)} %enc_ref.71, bf16[16384,896]{1,0:T(8,128)(2,1)} %dec_ref.71, s16[392,1024]{1,0:T(8,128)(2,1)} %stage0.10.refs_0_), custom_call_target="tpu_custom_call" | custom-call | flops 2305999872 | bytes 1 | tf_op jit(solution)/shard_map/stage0/pallas_call | solution.py:133
  40.2 3.7 %stage0.12.refs_1_ = s16[392,1024]{1,0:T(8,128)(2,1)S(1)} custom-call(s32[3]{0:T(128)S(1)} %shift-right-arithmetic_and_fusion.where_ref, bf16[2,192,896]{2,1,0:T(8,128)(2,1)S(1)} %maximum_select_fusion.rows_ref, bf16[896,16384]{1,0:T(8,128)(2,1)} %enc_ref.71, bf16[16384,896]{1,0:T(8,128)(2,1)} %dec_ref.71, s16[392,1024]{1,0:T(8,128)(2,1)S(1)} %stage0.11.refs_0_), custom_call_target="tpu_custom_call" | custom-call | flops 2305999872 | bytes 1 | tf_op jit(solution)/shard_map/stage0/pallas_call | solution.py:133
  44.5 4.2 %collective-permute-done.2.refs_0_ = s16[392,1024]{1,0:T(8,128)(2,1)S(1)} collective-permute-done((s16[392,1024]{1,0:T(8,128)(2,1)S(1)}, s16[392,1024]{1,0:T(8,128)(2,1)S(1)}, u32[]{:S(2)}, u32[]{:S(2)}) %collective-permute-start.2) | collective-permute-done | bytes 802848 | tf_op jit(solution)/shard_map/ppermute | solution.py:277
  48.7 2.8 %stage1.9.refs_1_ = s16[392,512]{1,0:T(8,128)(2,1)S(1)} custom-call(s32[3]{0:T(128)S(1)} %shift-right-arithmetic_and_fusion.where_ref, bf16[2,192,896]{2,1,0:T(8,128)(2,1)S(1)} %maximum_select_fusion.rows_ref, bf16[896,16384]{1,0:T(8,128)(2,1)} %enc_ref.71, bf16[16384,896]{1,0:T(8,128)(2,1)} %dec_ref.71, ...), custom_call_target="tpu_custom_call" | custom-call | flops 2305999872 | bytes 1 | tf_op jit(solution)/shard_map/stage1/pallas_call | solution.py:133
  57.4 3.7 %stage0.13.refs_2_ = s16[392,1024]{1,0:T(8,128)(2,1)S(1)} custom-call(s32[3]{0:T(128)S(1)} %shift-right-arithmetic_and_fusion.where_ref, bf16[2,192,896]{2,1,0:T(8,128)(2,1)S(1)} %maximum_select_fusion.rows_ref, bf16[896,16384]{1,0:T(8,128)(2,1)} %enc_ref.71, bf16[16384,896]{1,0:T(8,128)(2,1)} %dec_ref.71, s16[392,512]{1,0:T(8,128)(2,1)S(1)} %stage1.10.refs_0_), custom_call_target="tpu_custom_call" | custom-call | flops 2305999872 | bytes 1 | tf_op jit(solution)/shard_map/stage0/pallas_call | solution.py:133
  63.3 3.5 %collective-permute-done.4.refs_1_ = s16[392,512]{1,0:T(8,128)(2,1)S(1)} collective-permute-done((s16[392,512]{1,0:T(8,128)(2,1)S(1)}, s16[392,512]{1,0:T(8,128)(2,1)S(1)}, u32[]{:S(2)}, u32[]{:S(2)}) %collective-permute-start.4) | collective-permute-done | bytes 401440 | tf_op jit(solution)/shard_map/ppermute | solution.py:277
  69.3 2.8 %stage1.11.refs_2_ = s16[392,512]{1,0:T(8,128)(2,1)S(1)} custom-call(s32[3]{0:T(128)S(1)} %shift-right-arithmetic_and_fusion.where_ref, bf16[2,192,896]{2,1,0:T(8,128)(2,1)S(1)} %maximum_select_fusion.rows_ref, bf16[896,16384]{1,0:T(8,128)(2,1)} %enc_ref.71, bf16[16384,896]{1,0:T(8,128)(2,1)} %dec_ref.71, ...), custom_call_target="tpu_custom_call" | custom-call | flops 2305999872 | bytes 1 | tf_op jit(solution)/shard_map/stage1/pallas_call | solution.py:133
  74.6 3.6 %collective-permute-done.6.refs_1_ = s16[392,512]{1,0:T(8,128)(2,1)S(1)} collective-permute-done((s16[392,512]{1,0:T(8,128)(2,1)S(1)}, s16[392,512]{1,0:T(8,128)(2,1)S(1)}, u32[]{:S(2)}, u32[]{:S(2)}) %collective-permute-start.6) | collective-permute-done | bytes 401440 | tf_op jit(solution)/shard_map/ppermute | solution.py:277
  81.0 3.7 %stage0.14.refs_1_ = s16[392,1024]{1,0:T(8,128)(2,1)S(1)} custom-call(s32[3]{0:T(128)S(1)} %shift-right-arithmetic_and_fusion.where_ref, bf16[2,192,896]{2,1,0:T(8,128)(2,1)S(1)} %maximum_select_fusion.rows_ref, bf16[896,16384]{1,0:T(8,128)(2,1)} %enc_ref.71, bf16[16384,896]{1,0:T(8,128)(2,1)} %dec_ref.71, s16[392,256]{1,0:T(8,128)(2,1)S(1)} %stage2.10.refs_0_), custom_call_target="tpu_custom_call" | custom-call | flops 2305999872 | bytes 1 | tf_op jit(solution)/shard_map/stage0/pallas_call | solution.py:133
  94.9 2.8 %stage1.13.refs_0_ = s16[392,512]{1,0:T(8,128)(2,1)S(1)} custom-call(s32[3]{0:T(128)S(1)} %shift-right-arithmetic_and_fusion.where_ref, bf16[2,192,896]{2,1,0:T(8,128)(2,1)S(1)} %maximum_select_fusion.rows_ref, bf16[896,16384]{1,0:T(8,128)(2,1)} %enc_ref.71, bf16[16384,896]{1,0:T(8,128)(2,1)} %dec_ref.71, ...), custom_call_target="tpu_custom_call" | custom-call | flops 2305999872 | bytes 1 | tf_op jit(solution)/shard_map/stage1/pallas_call | solution.py:133
  98.3 4.3 %stage0.15.refs_2_ = s16[392,1024]{1,0:T(8,128)(2,1)} custom-call(s32[3]{0:T(128)S(1)} %shift-right-arithmetic_and_fusion.where_ref, bf16[2,192,896]{2,1,0:T(8,128)(2,1)S(1)} %maximum_select_fusion.rows_ref, bf16[896,16384]{1,0:T(8,128)(2,1)} %enc_ref.71, bf16[16384,896]{1,0:T(8,128)(2,1)} %dec_ref.71, s16[392,512]{1,0:T(8,128)(2,1)S(1)} %stage1.13.refs_0_), custom_call_target="tpu_custom_call" | custom-call | flops 2305999872 | bytes 1 | tf_op jit(solution)/shard_map/stage0/pallas_call | solution.py:133
  106.3 3.4 %collective-permute-start.19 = (s16[392,256]{1,0:T(8,128)(2,1)S(1)}, s16[392,256]{1,0:T(8,128)(2,1)S(1)}, u32[]{:S(2)}, u32[]{:S(2)}) collective-permute-start(s16[392,256]{1,0:T(8,128)(2,1)S(1)} %stage2.11.refs_1_), channel_id=1, source_target_pairs={{0,16},{4,20},{8,24},{12,28},{16,0},{20,4},{24,8},{28,12},{1,17},{... | collective-permute-start | bytes 602120 | tf_op jit(solution)/shard_map/ppermute | solution.py:277
  109.8 3.5 %stage1.14.refs_2_ = s16[392,512]{1,0:T(8,128)(2,1)} custom-call(s32[3]{0:T(128)S(1)} %shift-right-arithmetic_and_fusion.where_ref, bf16[2,192,896]{2,1,0:T(8,128)(2,1)S(1)} %maximum_select_fusion.rows_ref, bf16[896,16384]{1,0:T(8,128)(2,1)} %enc_ref.71, bf16[16384,896]{1,0:T(8,128)(2,1)} %dec_ref.71, s16[392,1024]{1,0:T(8,128)(2,1)S(1)} %collective-permute-done.12.refs_0_, ...), custom_call_target="tpu_custom_call" | custom-call | flops 2305999872 | bytes 1 | tf_op jit(solution)/shard_map/stage1/pallas_call | solution.py:133
  117.5 2.9 %stage2.13.refs_0_ = s16[392,256]{1,0:T(8,128)(2,1)} custom-call(s32[3]{0:T(128)S(1)} %shift-right-arithmetic_and_fusion.where_ref, bf16[2,192,896]{2,1,0:T(8,128)(2,1)S(1)} %maximum_select_fusion.rows_ref, bf16[896,16384]{1,0:T(8,128)(2,1)} %enc_ref.71, bf16[16384,896]{1,0:T(8,128)(2,1)} %dec_ref.71, s16[392,1024]{1,0:T(8,128)(2,1)S(1)} %collective-permute-done.3.refs_0_, ...), custom_call_target="tpu_custom_call" | custom-call | flops 2305999872 | bytes 1 | tf_op jit(solution)/shard_map/stage2/pallas_call | solution.py:133
  122.1 3.5 %stage0.16.refs_5_ = s16[392,512]{1,0:T(8,128)(2,1)} custom-call(s32[3]{0:T(128)S(1)} %shift-right-arithmetic_and_fusion.where_ref, bf16[2,192,896]{2,1,0:T(8,128)(2,1)S(1)} %maximum_select_fusion.rows_ref, bf16[896,16384]{1,0:T(8,128)(2,1)} %enc_ref.71, bf16[16384,896]{1,0:T(8,128)(2,1)} %dec_ref.71, s16[392,256]{1,0:T(8,128)(2,1)} %stage2.13.refs_0_), custom_call_target="tpu_custom_call" | custom-call | flops 2305999872 | bytes 1 | tf_op jit(solution)/shard_map/stage0/pallas_call | solution.py:133
  128.2 3.6 %collective-permute-done.18.refs_2_ = s16[392,256]{1,0:T(8,128)(2,1)S(1)} collective-permute-done((s16[392,256]{1,0:T(8,128)(2,1)S(1)}, s16[392,256]{1,0:T(8,128)(2,1)S(1)}, u32[]{:S(2)}, u32[]{:S(2)}) %collective-permute-start.18) | collective-permute-done | bytes 200736 | tf_op jit(solution)/shard_map/ppermute | solution.py:277
  135.3 4.2 %all-to-all-start.1 = ((s16[8,32,1152]{2,1,0:T(8,128)(2,1)}), s16[8,32,1152]{2,1,0:T(8,128)(2,1)}, u32[]{:S(2)}, u32[]{:S(2)}) async-start(s16[8,32,1152]{2,1,0:T(8,128)(2,1)} %bitcast.38), calls=%async_computation.1 | async-start | bytes 1179648 | tf_op jit(solution)/shard_map/all_to_all | solution.py:188
  144.2 3.5 %stage1.15.refs_2_ = s16[392,512]{1,0:T(8,128)(2,1)} custom-call(s32[3]{0:T(128)S(1)} %shift-right-arithmetic_and_fusion.where_ref, bf16[2,192,896]{2,1,0:T(8,128)(2,1)S(1)} %maximum_select_fusion.rows_ref, bf16[896,16384]{1,0:T(8,128)(2,1)} %enc_ref.71, bf16[16384,896]{1,0:T(8,128)(2,1)} %dec_ref.71, s16[392,1024]{1,0:T(8,128)(2,1)S(1)} %collective-permute-done.17.refs_0_, ...), custom_call_target="tpu_custom_call" | custom-call | flops 2305999872 | bytes 1 | tf_op jit(solution)/shard_map/stage1/pallas_call | solution.py:133
  153.9 2.9 %stage1.16.refs_5_ = s16[392,256]{1,0:T(8,128)(2,1)} custom-call(s32[3]{0:T(128)S(1)} %shift-right-arithmetic_and_fusion.where_ref, bf16[2,192,896]{2,1,0:T(8,128)(2,1)S(1)} %maximum_select_fusion.rows_ref, bf16[896,16384]{1,0:T(8,128)(2,1)} %enc_ref.71, bf16[16384,896]{1,0:T(8,128)(2,1)} %dec_ref.71, s16[392,512]{1,0:T(8,128)(2,1)} %collective-permute-done.15.refs_0_, ...), custom_call_target="tpu_custom_call" | custom-call | flops 2305999872 | bytes 1 | tf_op jit(solution)/shard_map/stage1/pallas_call | solution.py:133
  188.8 15.8 %all_to_all.23.whole_ref = s16[8,32,1152]{2,1,0:T(8,128)(2,1)S(1)} all-to-all(s16[8,32,1152]{2,1,0:T(8,128)(2,1)S(1)} %bitcast.37), channel_id=1, replica_groups=mesh['dp'=8,'feat'=4] {'dp'}, dimensions={0} | all-to-all | bytes 1179648 | tf_op jit(solution)/shard_map/all_to_all | solution.py:188
  (147 shorter events, 98.0 us)
Async XLA Ops:
  3.4 18.9 %all-to-all-start = ((bf16[8,24,1024]{2,1,0:T(8,128)(2,1)}), bf16[8,24,1024]{2,1,0:T(8,128)(2,1)S(1)}, u32[]{:S(2)}, u32[]{:S(2)}) async-start(bf16[8,24,1024]{2,1,0:T(8,128)(2,1)} %maximum_bitcast_fusion), calls=%async_computation | async-start | bytes 786432 | tf_op jit(solution)/shard_map/all_to_all | solution.py:243
  27.9 20.8 %collective-permute-start.2 = (s16[392,1024]{1,0:T(8,128)(2,1)S(1)}, s16[392,1024]{1,0:T(8,128)(2,1)S(1)}, u32[]{:S(2)}, u32[]{:S(2)}) collective-permute-start(s16[392,1024]{1,0:T(8,128)(2,1)S(1)} %stage0.9.refs_0_), channel_id=1, source_target_pairs={{0,4},{4,0},{8,12},{12,8},{16,20},{20,16},{24,28},{28,24},{1,5},{5... | collective-permute-start | bytes 2408456 | tf_op jit(solution)/shard_map/ppermute | solution.py:277
  33.7 20.8 %collective-permute-start.1 = (s16[392,1024]{1,0:T(8,128)(2,1)}, s16[392,1024]{1,0:T(8,128)(2,1)S(1)}, u32[]{:S(2)}, u32[]{:S(2)}) collective-permute-start(s16[392,1024]{1,0:T(8,128)(2,1)} %stage0.10.refs_0_), channel_id=1, source_target_pairs={{0,8},{4,12},{8,0},{12,4},{16,24},{20,28},{24,16},{28,20},{1,9},{5... | collective-permute-start | bytes 2408456 | tf_op jit(solution)/shard_map/ppermute | solution.py:277
  38.7 30.6 %collective-permute-start.7 = (s16[392,1024]{1,0:T(8,128)(2,1)S(1)}, s16[392,1024]{1,0:T(8,128)(2,1)S(1)}, u32[]{:S(2)}, u32[]{:S(2)}) collective-permute-start(s16[392,1024]{1,0:T(8,128)(2,1)S(1)} %stage0.11.refs_0_), channel_id=1, source_target_pairs={{0,4},{4,0},{8,12},{12,8},{16,20},{20,16},{24,28},{28,24},{1,5},{5... | collective-permute-start | bytes 2408456 | tf_op jit(solution)/shard_map/ppermute | solution.py:277
  43.9 40.9 %collective-permute-start.9 = (s16[392,1024]{1,0:T(8,128)(2,1)S(1)}, s16[392,1024]{1,0:T(8,128)(2,1)S(1)}, u32[]{:S(2)}, u32[]{:S(2)}) collective-permute-start(s16[392,1024]{1,0:T(8,128)(2,1)S(1)} %stage0.12.refs_1_), channel_id=1, source_target_pairs={{0,4},{4,0},{8,12},{12,8},{16,20},{20,16},{24,28},{28,24},{1,5},{5... | collective-permute-start | bytes 2408456 | tf_op jit(solution)/shard_map/ppermute | solution.py:277
  51.4 15.4 %collective-permute-start.4 = (s16[392,512]{1,0:T(8,128)(2,1)S(1)}, s16[392,512]{1,0:T(8,128)(2,1)S(1)}, u32[]{:S(2)}, u32[]{:S(2)}) collective-permute-start(s16[392,512]{1,0:T(8,128)(2,1)S(1)} %stage1.9.refs_1_), channel_id=1, source_target_pairs={{0,8},{4,12},{8,0},{12,4},{16,24},{20,28},{24,16},{28,20},{1,9},{5... | collective-permute-start | bytes 1204232 | tf_op jit(solution)/shard_map/ppermute | solution.py:277
  57.3 20.9 %collective-permute-start.6 = (s16[392,512]{1,0:T(8,128)(2,1)S(1)}, s16[392,512]{1,0:T(8,128)(2,1)S(1)}, u32[]{:S(2)}, u32[]{:S(2)}) collective-permute-start(s16[392,512]{1,0:T(8,128)(2,1)S(1)} %stage1.10.refs_0_), channel_id=1, source_target_pairs={{0,16},{4,20},{8,24},{12,28},{16,0},{20,4},{24,8},{28,12},{1,17},{... | collective-permute-start | bytes 1204232 | tf_op jit(solution)/shard_map/ppermute | solution.py:277
  61.1 33.9 %collective-permute-start.3 = (s16[392,1024]{1,0:T(8,128)(2,1)S(1)}, s16[392,1024]{1,0:T(8,128)(2,1)S(1)}, u32[]{:S(2)}, u32[]{:S(2)}) collective-permute-start(s16[392,1024]{1,0:T(8,128)(2,1)S(1)} %stage0.13.refs_2_), channel_id=1, source_target_pairs={{0,8},{4,12},{8,0},{12,4},{16,24},{20,28},{24,16},{28,20},{1,9},{5... | collective-permute-start | bytes 2408456 | tf_op jit(solution)/shard_map/ppermute | solution.py:277
  69.0 23.3 %collective-permute-start.5 = (s16[392,256]{1,0:T(8,128)(2,1)S(1)}, s16[392,256]{1,0:T(8,128)(2,1)S(1)}, u32[]{:S(2)}, u32[]{:S(2)}) collective-permute-start(s16[392,256]{1,0:T(8,128)(2,1)S(1)} %stage2.9.refs_1_), channel_id=1, source_target_pairs={{0,16},{4,20},{8,24},{12,28},{16,0},{20,4},{24,8},{28,12},{1,17},{... | collective-permute-start | bytes 602120 | tf_op jit(solution)/shard_map/ppermute | solution.py:277
  72.0 32.1 %collective-permute-start.13 = (s16[392,512]{1,0:T(8,128)(2,1)S(1)}, s16[392,512]{1,0:T(8,128)(2,1)S(1)}, u32[]{:S(2)}, u32[]{:S(2)}) collective-permute-start(s16[392,512]{1,0:T(8,128)(2,1)S(1)} %stage1.11.refs_2_), channel_id=1, source_target_pairs={{0,8},{4,12},{8,0},{12,4},{16,24},{20,28},{24,16},{28,20},{1,9},{5... | collective-permute-start | bytes 1204232 | tf_op jit(solution)/shard_map/ppermute | solution.py:277
  84.7 25.0 %collective-permute-start.12 = (s16[392,1024]{1,0:T(8,128)(2,1)S(1)}, s16[392,1024]{1,0:T(8,128)(2,1)S(1)}, u32[]{:S(2)}, u32[]{:S(2)}) collective-permute-start(s16[392,1024]{1,0:T(8,128)(2,1)S(1)} %stage0.14.refs_1_), channel_id=1, source_target_pairs={{0,4},{4,0},{8,12},{12,8},{16,20},{20,16},{24,28},{28,24},{1,5},{5... | collective-permute-start | bytes 2408456 | tf_op jit(solution)/shard_map/ppermute | solution.py:277
  89.0 25.0 %collective-permute-start.11 = (s16[392,512]{1,0:T(8,128)(2,1)S(1)}, s16[392,512]{1,0:T(8,128)(2,1)S(1)}, u32[]{:S(2)}, u32[]{:S(2)}) collective-permute-start(s16[392,512]{1,0:T(8,128)(2,1)S(1)} %stage1.12.refs_5_), channel_id=1, source_target_pairs={{0,8},{4,12},{8,0},{12,4},{16,24},{20,28},{24,16},{28,20},{1,9},{5... | collective-permute-start | bytes 1204232 | tf_op jit(solution)/shard_map/ppermute | solution.py:277
  97.7 19.8 %collective-permute-start.10 = (s16[392,512]{1,0:T(8,128)(2,1)S(1)}, s16[392,512]{1,0:T(8,128)(2,1)S(1)}, u32[]{:S(2)}, u32[]{:S(2)}) collective-permute-start(s16[392,512]{1,0:T(8,128)(2,1)S(1)} %stage1.13.refs_0_), channel_id=1, source_target_pairs={{0,4},{4,0},{8,12},{12,8},{16,20},{20,16},{24,28},{28,24},{1,5},{5... | collective-permute-start | bytes 1204232 | tf_op jit(solution)/shard_map/ppermute | solution.py:277
  102.6 41.6 %collective-permute-start.17 = (s16[392,1024]{1,0:T(8,128)(2,1)}, s16[392,1024]{1,0:T(8,128)(2,1)S(1)}, u32[]{:S(2)}, u32[]{:S(2)}) collective-permute-start(s16[392,1024]{1,0:T(8,128)(2,1)} %stage0.15.refs_2_), channel_id=1, source_target_pairs={{0,4},{4,0},{8,12},{12,8},{16,20},{20,16},{24,28},{28,24},{1,5},{5... | collective-permute-start | bytes 2408456 | tf_op jit(solution)/shard_map/ppermute | solution.py:277
  106.3 19.3 %collective-permute-start.19 = (s16[392,256]{1,0:T(8,128)(2,1)S(1)}, s16[392,256]{1,0:T(8,128)(2,1)S(1)}, u32[]{:S(2)}, u32[]{:S(2)}) collective-permute-start(s16[392,256]{1,0:T(8,128)(2,1)S(1)} %stage2.11.refs_1_), channel_id=1, source_target_pairs={{0,16},{4,20},{8,24},{12,28},{16,0},{20,4},{24,8},{28,12},{1,17},{... | collective-permute-start | bytes 602120 | tf_op jit(solution)/shard_map/ppermute | solution.py:277
  113.3 35.9 %collective-permute-start.16 = (s16[392,512]{1,0:T(8,128)(2,1)}, s16[392,512]{1,0:T(8,128)(2,1)}, u32[]{:S(2)}, u32[]{:S(2)}) collective-permute-start(s16[392,512]{1,0:T(8,128)(2,1)} %stage1.14.refs_2_), channel_id=1, source_target_pairs={{0,8},{4,12},{8,0},{12,4},{16,24},{20,28},{24,16},{28,20},{1,9},{5... | collective-permute-start | bytes 1204232 | tf_op jit(solution)/shard_map/ppermute | solution.py:277
  116.2 15.5 %collective-permute-start.18 = (s16[392,256]{1,0:T(8,128)(2,1)S(1)}, s16[392,256]{1,0:T(8,128)(2,1)S(1)}, u32[]{:S(2)}, u32[]{:S(2)}) collective-permute-start(s16[392,256]{1,0:T(8,128)(2,1)S(1)} %stage2.12.refs_2_), channel_id=1, source_target_pairs={{0,16},{4,20},{8,24},{12,28},{16,0},{20,4},{24,8},{28,12},{1,17},{... | collective-permute-start | bytes 602120 | tf_op jit(solution)/shard_map/ppermute | solution.py:277
  120.4 37.0 %collective-permute-start.14 = (s16[392,256]{1,0:T(8,128)(2,1)}, s16[392,256]{1,0:T(8,128)(2,1)}, u32[]{:S(2)}, u32[]{:S(2)}) collective-permute-start(s16[392,256]{1,0:T(8,128)(2,1)} %stage2.13.refs_0_), channel_id=1, source_target_pairs={{0,16},{4,20},{8,24},{12,28},{16,0},{20,4},{24,8},{28,12},{1,17},{... | collective-permute-start | bytes 602120 | tf_op jit(solution)/shard_map/ppermute | solution.py:277
  125.6 28.3 %collective-permute-start.15 = (s16[392,512]{1,0:T(8,128)(2,1)}, s16[392,512]{1,0:T(8,128)(2,1)}, u32[]{:S(2)}, u32[]{:S(2)}) collective-permute-start(s16[392,512]{1,0:T(8,128)(2,1)} %stage0.16.refs_5_), channel_id=1, source_target_pairs={{0,4},{4,0},{8,12},{12,8},{16,20},{20,16},{24,28},{28,24},{1,5},{5... | collective-permute-start | bytes 1204232 | tf_op jit(solution)/shard_map/ppermute | solution.py:277
  135.3 28.3 %all-to-all-start.1 = ((s16[8,32,1152]{2,1,0:T(8,128)(2,1)}), s16[8,32,1152]{2,1,0:T(8,128)(2,1)}, u32[]{:S(2)}, u32[]{:S(2)}) async-start(s16[8,32,1152]{2,1,0:T(8,128)(2,1)} %bitcast.38), calls=%async_computation.1 | async-start | bytes 1179648 | tf_op jit(solution)/shard_map/all_to_all | solution.py:188
  142.2 18.5 %collective-permute-start.21 = (s16[392,512]{1,0:T(8,128)(2,1)S(1)}, s16[392,512]{1,0:T(8,128)(2,1)S(1)}, u32[]{:S(2)}, u32[]{:S(2)}) collective-permute-start(s16[392,512]{1,0:T(8,128)(2,1)S(1)} %stage0.17.refs_1_), channel_id=1, source_target_pairs={{0,4},{4,0},{8,12},{12,8},{16,20},{20,16},{24,28},{28,24},{1,5},{5... | collective-permute-start | bytes 1204232 | tf_op jit(solution)/shard_map/ppermute | solution.py:277
  147.7 18.7 %collective-permute-start.24 = (s16[392,512]{1,0:T(8,128)(2,1)}, s16[392,512]{1,0:T(8,128)(2,1)}, u32[]{:S(2)}, u32[]{:S(2)}) collective-permute-start(s16[392,512]{1,0:T(8,128)(2,1)} %stage1.15.refs_2_), channel_id=1, source_target_pairs={{0,8},{4,12},{8,0},{12,4},{16,24},{20,28},{24,16},{28,20},{1,9},{5... | collective-permute-start | bytes 1204232 | tf_op jit(solution)/shard_map/ppermute | solution.py:277
  151.5 26.9 %collective-permute-start.20 = (s16[392,256]{1,0:T(8,128)(2,1)S(1)}, s16[392,256]{1,0:T(8,128)(2,1)}, u32[]{:S(2)}, u32[]{:S(2)}) collective-permute-start(s16[392,256]{1,0:T(8,128)(2,1)S(1)} %stage2.14.refs_1_), channel_id=1, source_target_pairs={{0,16},{4,20},{8,24},{12,28},{16,0},{20,4},{24,8},{28,12},{1,17},{... | collective-permute-start | bytes 602120 | tf_op jit(solution)/shard_map/ppermute | solution.py:277
  156.9 15.2 %collective-permute-start.23 = (s16[392,256]{1,0:T(8,128)(2,1)}, s16[392,256]{1,0:T(8,128)(2,1)}, u32[]{:S(2)}, u32[]{:S(2)}) collective-permute-start(s16[392,256]{1,0:T(8,128)(2,1)} %stage1.16.refs_5_), channel_id=1, source_target_pairs={{0,16},{4,20},{8,24},{12,28},{16,0},{20,4},{24,8},{28,12},{1,17},{... | collective-permute-start | bytes 602120 | tf_op jit(solution)/shard_map/ppermute | solution.py:277
  (27 other events, 135.1 us)

commit v4 on v3

--- a/solution.py
+++ b/solution.py
@@ -216,7 +216,7 @@
     (7, 0), (2, 3), (3, 3), (8, 0), (6, 1), (5, 2), (7, 1), (4, 3), (8, 1), (-1, 0),
     (6, 2), (7, 2), (8, 2), (5, 3), (7, 3), (6, 3), (8, 3),
 ]
-COSTS = [2306000000]
+COSTS = [2306000000] * 31 + [576500000] * 6
 
 
 def route_table(routes):

time: 207 us -> 207 us (level)
  no operation moved by 1% of the time
where the time goes in v4:
time: 207 us; the launch traced here: 206 us
  Pallas kernels  106 us (51%)
  starting transfers between devices  43.1 us (21%)
  waiting for transfers between devices  30.5 us (15%)
  blocking collectives  15.8 us (8%)
  other arithmetic  6.4 us (3%)
  local copies, waits for them, and re-layouts  3.54 us (2%)
    pallas_call x36, Pallas kernels, run_stage(): pl.pallas_call(functools.partial(body, tokens, len(chunk.messages)), grid...  102 us
    ppermute x27, starting transfers between devices, on_device(): chunk.messages.append(lax.ppermute(result, 'dp', partner))  31.6 us
    ppermute x27, waiting for transfers between devices, on_device(): chunk.messages.append(lax.ppermute(result, 'dp', partner))  19 us
    all_to_all x1, blocking collectives, collect(): whole = lax.all_to_all(whole, 'dp', split_axis=0, concat_axis=0, tiled=True)  15.8 us
    all_to_all x1, waiting for transfers between devices, gather_rows(): got = lax.all_to_all(own, 'dp', split_axis=0, concat_axis=0, tiled=True)  9.98 us
    all_to_all x1, starting transfers between devices, gather_rows(): got = lax.all_to_all(own, 'dp', split_axis=0, concat_axis=0, tiled=True)  7.25 us
    all_to_all x1, starting transfers between devices, collect(): whole = lax.all_to_all(whole, 'dp', split_axis=0, concat_axis=0, tiled=True)  4.2 us
  transfers between devices with their start and end apart: 30, of which 10 were waited for; matrix products, arithmetic and copies ran while one was open for 2% of the time, Pallas kernels for 48%

profile of v4, /device:TPU:0, one launch (start us, length us, event | category | flops | bytes accessed | tf_op | source)
XLA Modules:
  0.0 205.8 jit_solution(14337311135625394823)
XLA Ops:
  3.4 7.3 %all-to-all-start = ((bf16[8,24,1024]{2,1,0:T(8,128)(2,1)}), bf16[8,24,1024]{2,1,0:T(8,128)(2,1)S(1)}, u32[]{:S(2)}, u32[]{:S(2)}) async-start(bf16[8,24,1024]{2,1,0:T(8,128)(2,1)} %maximum_bitcast_fusion), calls=%async_computation | async-start | bytes 786432 | tf_op jit(solution)/shard_map/all_to_all | solution.py:243
  12.3 10.0 %all-to-all-done = bf16[8,24,1024]{2,1,0:T(8,128)(2,1)S(1)} async-done(((bf16[8,24,1024]{2,1,0:T(8,128)(2,1)}), bf16[8,24,1024]{2,1,0:T(8,128)(2,1)S(1)}, u32[]{:S(2)}, u32[]{:S(2)}) %all-to-all-start) | async-done | bytes 393248 | tf_op jit(solution)/shard_map/all_to_all | solution.py:243
  24.2 3.7 %stage0.9.refs_0_ = s16[392,1024]{1,0:T(8,128)(2,1)S(1)} custom-call(s32[3]{0:T(128)S(1)} %shift-right-arithmetic_and_fusion.where_ref, bf16[2,192,896]{2,1,0:T(8,128)(2,1)S(1)} %maximum_select_fusion.rows_ref, bf16[896,16384]{1,0:T(8,128)(2,1)} %enc_ref.71, bf16[16384,896]{1,0:T(8,128)(2,1)} %dec_ref.71), custom_call_target="tpu_custom_call" | custom-call | flops 2305999872 | bytes 1 | tf_op jit(solution)/shard_map/stage0/pallas_call | solution.py:133
  29.4 4.3 %stage0.10.refs_0_ = s16[392,1024]{1,0:T(8,128)(2,1)} custom-call(s32[3]{0:T(128)S(1)} %shift-right-arithmetic_and_fusion.where_ref, bf16[2,192,896]{2,1,0:T(8,128)(2,1)S(1)} %maximum_select_fusion.rows_ref, bf16[896,16384]{1,0:T(8,128)(2,1)} %enc_ref.71, bf16[16384,896]{1,0:T(8,128)(2,1)} %dec_ref.71, s16[392,1024]{1,0:T(8,128)(2,1)S(1)} %stage0.9.refs_0_), custom_call_target="tpu_custom_call" | custom-call | flops 2305999872 | bytes 1 | tf_op jit(solution)/shard_map/stage0/pallas_call | solution.py:133
  35.0 3.7 %stage0.11.refs_0_ = s16[392,1024]{1,0:T(8,128)(2,1)S(1)} custom-call(s32[3]{0:T(128)S(1)} %shift-right-arithmetic_and_fusion.where_ref, bf16[2,192,896]{2,1,0:T(8,128)(2,1)S(1)} %maximum_select_fusion.rows_ref, bf16[896,16384]{1,0:T(8,128)(2,1)} %enc_ref.71, bf16[16384,896]{1,0:T(8,128)(2,1)} %dec_ref.71, s16[392,1024]{1,0:T(8,128)(2,1)} %stage0.10.refs_0_), custom_call_target="tpu_custom_call" | custom-call | flops 2305999872 | bytes 1 | tf_op jit(solution)/shard_map/stage0/pallas_call | solution.py:133
  40.2 3.7 %stage0.12.refs_1_ = s16[392,1024]{1,0:T(8,128)(2,1)S(1)} custom-call(s32[3]{0:T(128)S(1)} %shift-right-arithmetic_and_fusion.where_ref, bf16[2,192,896]{2,1,0:T(8,128)(2,1)S(1)} %maximum_select_fusion.rows_ref, bf16[896,16384]{1,0:T(8,128)(2,1)} %enc_ref.71, bf16[16384,896]{1,0:T(8,128)(2,1)} %dec_ref.71, s16[392,1024]{1,0:T(8,128)(2,1)S(1)} %stage0.11.refs_0_), custom_call_target="tpu_custom_call" | custom-call | flops 2305999872 | bytes 1 | tf_op jit(solution)/shard_map/stage0/pallas_call | solution.py:133
  44.5 4.2 %collective-permute-done.2.refs_0_ = s16[392,1024]{1,0:T(8,128)(2,1)S(1)} collective-permute-done((s16[392,1024]{1,0:T(8,128)(2,1)S(1)}, s16[392,1024]{1,0:T(8,128)(2,1)S(1)}, u32[]{:S(2)}, u32[]{:S(2)}) %collective-permute-start.2) | collective-permute-done | bytes 802848 | tf_op jit(solution)/shard_map/ppermute | solution.py:277
  48.7 2.8 %stage1.9.refs_1_ = s16[392,512]{1,0:T(8,128)(2,1)S(1)} custom-call(s32[3]{0:T(128)S(1)} %shift-right-arithmetic_and_fusion.where_ref, bf16[2,192,896]{2,1,0:T(8,128)(2,1)S(1)} %maximum_select_fusion.rows_ref, bf16[896,16384]{1,0:T(8,128)(2,1)} %enc_ref.71, bf16[16384,896]{1,0:T(8,128)(2,1)} %dec_ref.71, ...), custom_call_target="tpu_custom_call" | custom-call | flops 2305999872 | bytes 1 | tf_op jit(solution)/shard_map/stage1/pallas_call | solution.py:133
  57.4 3.7 %stage0.13.refs_2_ = s16[392,1024]{1,0:T(8,128)(2,1)S(1)} custom-call(s32[3]{0:T(128)S(1)} %shift-right-arithmetic_and_fusion.where_ref, bf16[2,192,896]{2,1,0:T(8,128)(2,1)S(1)} %maximum_select_fusion.rows_ref, bf16[896,16384]{1,0:T(8,128)(2,1)} %enc_ref.71, bf16[16384,896]{1,0:T(8,128)(2,1)} %dec_ref.71, s16[392,512]{1,0:T(8,128)(2,1)S(1)} %stage1.10.refs_0_), custom_call_target="tpu_custom_call" | custom-call | flops 2305999872 | bytes 1 | tf_op jit(solution)/shard_map/stage0/pallas_call | solution.py:133
  63.3 3.5 %collective-permute-done.4.refs_1_ = s16[392,512]{1,0:T(8,128)(2,1)S(1)} collective-permute-done((s16[392,512]{1,0:T(8,128)(2,1)S(1)}, s16[392,512]{1,0:T(8,128)(2,1)S(1)}, u32[]{:S(2)}, u32[]{:S(2)}) %collective-permute-start.4) | collective-permute-done | bytes 401440 | tf_op jit(solution)/shard_map/ppermute | solution.py:277
  69.3 2.8 %stage1.11.refs_2_ = s16[392,512]{1,0:T(8,128)(2,1)S(1)} custom-call(s32[3]{0:T(128)S(1)} %shift-right-arithmetic_and_fusion.where_ref, bf16[2,192,896]{2,1,0:T(8,128)(2,1)S(1)} %maximum_select_fusion.rows_ref, bf16[896,16384]{1,0:T(8,128)(2,1)} %enc_ref.71, bf16[16384,896]{1,0:T(8,128)(2,1)} %dec_ref.71, ...), custom_call_target="tpu_custom_call" | custom-call | flops 2305999872 | bytes 1 | tf_op jit(solution)/shard_map/stage1/pallas_call | solution.py:133
  74.6 3.6 %collective-permute-done.6.refs_1_ = s16[392,512]{1,0:T(8,128)(2,1)S(1)} collective-permute-done((s16[392,512]{1,0:T(8,128)(2,1)S(1)}, s16[392,512]{1,0:T(8,128)(2,1)S(1)}, u32[]{:S(2)}, u32[]{:S(2)}) %collective-permute-start.6) | collective-permute-done | bytes 401440 | tf_op jit(solution)/shard_map/ppermute | solution.py:277
  81.0 3.7 %stage0.14.refs_1_ = s16[392,1024]{1,0:T(8,128)(2,1)S(1)} custom-call(s32[3]{0:T(128)S(1)} %shift-right-arithmetic_and_fusion.where_ref, bf16[2,192,896]{2,1,0:T(8,128)(2,1)S(1)} %maximum_select_fusion.rows_ref, bf16[896,16384]{1,0:T(8,128)(2,1)} %enc_ref.71, bf16[16384,896]{1,0:T(8,128)(2,1)} %dec_ref.71, s16[392,256]{1,0:T(8,128)(2,1)S(1)} %stage2.10.refs_0_), custom_call_target="tpu_custom_call" | custom-call | flops 2305999872 | bytes 1 | tf_op jit(solution)/shard_map/stage0/pallas_call | solution.py:133
  94.9 2.8 %stage1.13.refs_0_ = s16[392,512]{1,0:T(8,128)(2,1)S(1)} custom-call(s32[3]{0:T(128)S(1)} %shift-right-arithmetic_and_fusion.where_ref, bf16[2,192,896]{2,1,0:T(8,128)(2,1)S(1)} %maximum_select_fusion.rows_ref, bf16[896,16384]{1,0:T(8,128)(2,1)} %enc_ref.71, bf16[16384,896]{1,0:T(8,128)(2,1)} %dec_ref.71, ...), custom_call_target="tpu_custom_call" | custom-call | flops 2305999872 | bytes 1 | tf_op jit(solution)/shard_map/stage1/pallas_call | solution.py:133
  98.3 4.3 %stage0.15.refs_2_ = s16[392,1024]{1,0:T(8,128)(2,1)} custom-call(s32[3]{0:T(128)S(1)} %shift-right-arithmetic_and_fusion.where_ref, bf16[2,192,896]{2,1,0:T(8,128)(2,1)S(1)} %maximum_select_fusion.rows_ref, bf16[896,16384]{1,0:T(8,128)(2,1)} %enc_ref.71, bf16[16384,896]{1,0:T(8,128)(2,1)} %dec_ref.71, s16[392,512]{1,0:T(8,128)(2,1)S(1)} %stage1.13.refs_0_), custom_call_target="tpu_custom_call" | custom-call | flops 2305999872 | bytes 1 | tf_op jit(solution)/shard_map/stage0/pallas_call | solution.py:133
  106.3 3.4 %collective-permute-start.19 = (s16[392,256]{1,0:T(8,128)(2,1)S(1)}, s16[392,256]{1,0:T(8,128)(2,1)S(1)}, u32[]{:S(2)}, u32[]{:S(2)}) collective-permute-start(s16[392,256]{1,0:T(8,128)(2,1)S(1)} %stage2.11.refs_1_), channel_id=1, source_target_pairs={{0,16},{4,20},{8,24},{12,28},{16,0},{20,4},{24,8},{28,12},{1,17},{... | collective-permute-start | bytes 602120 | tf_op jit(solution)/shard_map/ppermute | solution.py:277
  109.8 3.5 %stage1.14.refs_2_ = s16[392,512]{1,0:T(8,128)(2,1)} custom-call(s32[3]{0:T(128)S(1)} %shift-right-arithmetic_and_fusion.where_ref, bf16[2,192,896]{2,1,0:T(8,128)(2,1)S(1)} %maximum_select_fusion.rows_ref, bf16[896,16384]{1,0:T(8,128)(2,1)} %enc_ref.71, bf16[16384,896]{1,0:T(8,128)(2,1)} %dec_ref.71, s16[392,1024]{1,0:T(8,128)(2,1)S(1)} %collective-permute-done.12.refs_0_, ...), custom_call_target="tpu_custom_call" | custom-call | flops 2305999872 | bytes 1 | tf_op jit(solution)/shard_map/stage1/pallas_call | solution.py:133
  117.5 2.9 %stage2.13.refs_0_ = s16[392,256]{1,0:T(8,128)(2,1)} custom-call(s32[3]{0:T(128)S(1)} %shift-right-arithmetic_and_fusion.where_ref, bf16[2,192,896]{2,1,0:T(8,128)(2,1)S(1)} %maximum_select_fusion.rows_ref, bf16[896,16384]{1,0:T(8,128)(2,1)} %enc_ref.71, bf16[16384,896]{1,0:T(8,128)(2,1)} %dec_ref.71, s16[392,1024]{1,0:T(8,128)(2,1)S(1)} %collective-permute-done.3.refs_0_, ...), custom_call_target="tpu_custom_call" | custom-call | flops 2305999872 | bytes 1 | tf_op jit(solution)/shard_map/stage2/pallas_call | solution.py:133
  122.1 3.5 %stage0.16.refs_5_ = s16[392,512]{1,0:T(8,128)(2,1)} custom-call(s32[3]{0:T(128)S(1)} %shift-right-arithmetic_and_fusion.where_ref, bf16[2,192,896]{2,1,0:T(8,128)(2,1)S(1)} %maximum_select_fusion.rows_ref, bf16[896,16384]{1,0:T(8,128)(2,1)} %enc_ref.71, bf16[16384,896]{1,0:T(8,128)(2,1)} %dec_ref.71, s16[392,256]{1,0:T(8,128)(2,1)} %stage2.13.refs_0_), custom_call_target="tpu_custom_call" | custom-call | flops 2305999872 | bytes 1 | tf_op jit(solution)/shard_map/stage0/pallas_call | solution.py:133
  128.2 3.6 %collective-permute-done.18.refs_2_ = s16[392,256]{1,0:T(8,128)(2,1)S(1)} collective-permute-done((s16[392,256]{1,0:T(8,128)(2,1)S(1)}, s16[392,256]{1,0:T(8,128)(2,1)S(1)}, u32[]{:S(2)}, u32[]{:S(2)}) %collective-permute-start.18) | collective-permute-done | bytes 200736 | tf_op jit(solution)/shard_map/ppermute | solution.py:277
  135.3 4.2 %all-to-all-start.1 = ((s16[8,32,1152]{2,1,0:T(8,128)(2,1)}), s16[8,32,1152]{2,1,0:T(8,128)(2,1)}, u32[]{:S(2)}, u32[]{:S(2)}) async-start(s16[8,32,1152]{2,1,0:T(8,128)(2,1)} %bitcast.38), calls=%async_computation.1 | async-start | bytes 1179648 | tf_op jit(solution)/shard_map/all_to_all | solution.py:188
  144.2 3.5 %stage1.15.refs_2_ = s16[392,512]{1,0:T(8,128)(2,1)} custom-call(s32[3]{0:T(128)S(1)} %shift-right-arithmetic_and_fusion.where_ref, bf16[2,192,896]{2,1,0:T(8,128)(2,1)S(1)} %maximum_select_fusion.rows_ref, bf16[896,16384]{1,0:T(8,128)(2,1)} %enc_ref.71, bf16[16384,896]{1,0:T(8,128)(2,1)} %dec_ref.71, s16[392,1024]{1,0:T(8,128)(2,1)S(1)} %collective-permute-done.17.refs_0_, ...), custom_call_target="tpu_custom_call" | custom-call | flops 2305999872 | bytes 1 | tf_op jit(solution)/shard_map/stage1/pallas_call | solution.py:133
  153.9 2.9 %stage1.16.refs_5_ = s16[392,256]{1,0:T(8,128)(2,1)} custom-call(s32[3]{0:T(128)S(1)} %shift-right-arithmetic_and_fusion.where_ref, bf16[2,192,896]{2,1,0:T(8,128)(2,1)S(1)} %maximum_select_fusion.rows_ref, bf16[896,16384]{1,0:T(8,128)(2,1)} %enc_ref.71, bf16[16384,896]{1,0:T(8,128)(2,1)} %dec_ref.71, s16[392,512]{1,0:T(8,128)(2,1)} %collective-permute-done.15.refs_0_, ...), custom_call_target="tpu_custom_call" | custom-call | flops 2305999872 | bytes 1 | tf_op jit(solution)/shard_map/stage1/pallas_call | solution.py:133
  188.8 15.8 %all_to_all.23.whole_ref = s16[8,32,1152]{2,1,0:T(8,128)(2,1)S(1)} all-to-all(s16[8,32,1152]{2,1,0:T(8,128)(2,1)S(1)} %bitcast.37), channel_id=1, replica_groups=mesh['dp'=8,'feat'=4] {'dp'}, dimensions={0} | all-to-all | bytes 1179648 | tf_op jit(solution)/shard_map/all_to_all | solution.py:188
  (147 shorter events, 98.0 us)
Async XLA Ops:
  3.4 18.9 %all-to-all-start = ((bf16[8,24,1024]{2,1,0:T(8,128)(2,1)}), bf16[8,24,1024]{2,1,0:T(8,128)(2,1)S(1)}, u32[]{:S(2)}, u32[]{:S(2)}) async-start(bf16[8,24,1024]{2,1,0:T(8,128)(2,1)} %maximum_bitcast_fusion), calls=%async_computation | async-start | bytes 786432 | tf_op jit(solution)/shard_map/all_to_all | solution.py:243
  27.9 20.8 %collective-permute-start.2 = (s16[392,1024]{1,0:T(8,128)(2,1)S(1)}, s16[392,1024]{1,0:T(8,128)(2,1)S(1)}, u32[]{:S(2)}, u32[]{:S(2)}) collective-permute-start(s16[392,1024]{1,0:T(8,128)(2,1)S(1)} %stage0.9.refs_0_), channel_id=1, source_target_pairs={{0,4},{4,0},{8,12},{12,8},{16,20},{20,16},{24,28},{28,24},{1,5},{5... | collective-permute-start | bytes 2408456 | tf_op jit(solution)/shard_map/ppermute | solution.py:277
  33.7 20.8 %collective-permute-start.1 = (s16[392,1024]{1,0:T(8,128)(2,1)}, s16[392,1024]{1,0:T(8,128)(2,1)S(1)}, u32[]{:S(2)}, u32[]{:S(2)}) collective-permute-start(s16[392,1024]{1,0:T(8,128)(2,1)} %stage0.10.refs_0_), channel_id=1, source_target_pairs={{0,8},{4,12},{8,0},{12,4},{16,24},{20,28},{24,16},{28,20},{1,9},{5... | collective-permute-start | bytes 2408456 | tf_op jit(solution)/shard_map/ppermute | solution.py:277
  38.7 30.6 %collective-permute-start.7 = (s16[392,1024]{1,0:T(8,128)(2,1)S(1)}, s16[392,1024]{1,0:T(8,128)(2,1)S(1)}, u32[]{:S(2)}, u32[]{:S(2)}) collective-permute-start(s16[392,1024]{1,0:T(8,128)(2,1)S(1)} %stage0.11.refs_0_), channel_id=1, source_target_pairs={{0,4},{4,0},{8,12},{12,8},{16,20},{20,16},{24,28},{28,24},{1,5},{5... | collective-permute-start | bytes 2408456 | tf_op jit(solution)/shard_map/ppermute | solution.py:277
  43.9 40.9 %collective-permute-start.9 = (s16[392,1024]{1,0:T(8,128)(2,1)S(1)}, s16[392,1024]{1,0:T(8,128)(2,1)S(1)}, u32[]{:S(2)}, u32[]{:S(2)}) collective-permute-start(s16[392,1024]{1,0:T(8,128)(2,1)S(1)} %stage0.12.refs_1_), channel_id=1, source_target_pairs={{0,4},{4,0},{8,12},{12,8},{16,20},{20,16},{24,28},{28,24},{1,5},{5... | collective-permute-start | bytes 2408456 | tf_op jit(solution)/shard_map/ppermute | solution.py:277
  51.4 15.4 %collective-permute-start.4 = (s16[392,512]{1,0:T(8,128)(2,1)S(1)}, s16[392,512]{1,0:T(8,128)(2,1)S(1)}, u32[]{:S(2)}, u32[]{:S(2)}) collective-permute-start(s16[392,512]{1,0:T(8,128)(2,1)S(1)} %stage1.9.refs_1_), channel_id=1, source_target_pairs={{0,8},{4,12},{8,0},{12,4},{16,24},{20,28},{24,16},{28,20},{1,9},{5... | collective-permute-start | bytes 1204232 | tf_op jit(solution)/shard_map/ppermute | solution.py:277
  57.3 20.9 %collective-permute-start.6 = (s16[392,512]{1,0:T(8,128)(2,1)S(1)}, s16[392,512]{1,0:T(8,128)(2,1)S(1)}, u32[]{:S(2)}, u32[]{:S(2)}) collective-permute-start(s16[392,512]{1,0:T(8,128)(2,1)S(1)} %stage1.10.refs_0_), channel_id=1, source_target_pairs={{0,16},{4,20},{8,24},{12,28},{16,0},{20,4},{24,8},{28,12},{1,17},{... | collective-permute-start | bytes 1204232 | tf_op jit(solution)/shard_map/ppermute | solution.py:277
  61.1 33.9 %collective-permute-start.3 = (s16[392,1024]{1,0:T(8,128)(2,1)S(1)}, s16[392,1024]{1,0:T(8,128)(2,1)S(1)}, u32[]{:S(2)}, u32[]{:S(2)}) collective-permute-start(s16[392,1024]{1,0:T(8,128)(2,1)S(1)} %stage0.13.refs_2_), channel_id=1, source_target_pairs={{0,8},{4,12},{8,0},{12,4},{16,24},{20,28},{24,16},{28,20},{1,9},{5... | collective-permute-start | bytes 2408456 | tf_op jit(solution)/shard_map/ppermute | solution.py:277
  69.0 23.3 %collective-permute-start.5 = (s16[392,256]{1,0:T(8,128)(2,1)S(1)}, s16[392,256]{1,0:T(8,128)(2,1)S(1)}, u32[]{:S(2)}, u32[]{:S(2)}) collective-permute-start(s16[392,256]{1,0:T(8,128)(2,1)S(1)} %stage2.9.refs_1_), channel_id=1, source_target_pairs={{0,16},{4,20},{8,24},{12,28},{16,0},{20,4},{24,8},{28,12},{1,17},{... | collective-permute-start | bytes 602120 | tf_op jit(solution)/shard_map/ppermute | solution.py:277
  72.0 32.1 %collective-permute-start.13 = (s16[392,512]{1,0:T(8,128)(2,1)S(1)}, s16[392,512]{1,0:T(8,128)(2,1)S(1)}, u32[]{:S(2)}, u32[]{:S(2)}) collective-permute-start(s16[392,512]{1,0:T(8,128)(2,1)S(1)} %stage1.11.refs_2_), channel_id=1, source_target_pairs={{0,8},{4,12},{8,0},{12,4},{16,24},{20,28},{24,16},{28,20},{1,9},{5... | collective-permute-start | bytes 1204232 | tf_op jit(solution)/shard_map/ppermute | solution.py:277
  84.7 25.0 %collective-permute-start.12 = (s16[392,1024]{1,0:T(8,128)(2,1)S(1)}, s16[392,1024]{1,0:T(8,128)(2,1)S(1)}, u32[]{:S(2)}, u32[]{:S(2)}) collective-permute-start(s16[392,1024]{1,0:T(8,128)(2,1)S(1)} %stage0.14.refs_1_), channel_id=1, source_target_pairs={{0,4},{4,0},{8,12},{12,8},{16,20},{20,16},{24,28},{28,24},{1,5},{5... | collective-permute-start | bytes 2408456 | tf_op jit(solution)/shard_map/ppermute | solution.py:277
  89.0 25.0 %collective-permute-start.11 = (s16[392,512]{1,0:T(8,128)(2,1)S(1)}, s16[392,512]{1,0:T(8,128)(2,1)S(1)}, u32[]{:S(2)}, u32[]{:S(2)}) collective-permute-start(s16[392,512]{1,0:T(8,128)(2,1)S(1)} %stage1.12.refs_5_), channel_id=1, source_target_pairs={{0,8},{4,12},{8,0},{12,4},{16,24},{20,28},{24,16},{28,20},{1,9},{5... | collective-permute-start | bytes 1204232 | tf_op jit(solution)/shard_map/ppermute | solution.py:277
  97.7 19.8 %collective-permute-start.10 = (s16[392,512]{1,0:T(8,128)(2,1)S(1)}, s16[392,512]{1,0:T(8,128)(2,1)S(1)}, u32[]{:S(2)}, u32[]{:S(2)}) collective-permute-start(s16[392,512]{1,0:T(8,128)(2,1)S(1)} %stage1.13.refs_0_), channel_id=1, source_target_pairs={{0,4},{4,0},{8,12},{12,8},{16,20},{20,16},{24,28},{28,24},{1,5},{5... | collective-permute-start | bytes 1204232 | tf_op jit(solution)/shard_map/ppermute | solution.py:277
  102.6 41.6 %collective-permute-start.17 = (s16[392,1024]{1,0:T(8,128)(2,1)}, s16[392,1024]{1,0:T(8,128)(2,1)S(1)}, u32[]{:S(2)}, u32[]{:S(2)}) collective-permute-start(s16[392,1024]{1,0:T(8,128)(2,1)} %stage0.15.refs_2_), channel_id=1, source_target_pairs={{0,4},{4,0},{8,12},{12,8},{16,20},{20,16},{24,28},{28,24},{1,5},{5... | collective-permute-start | bytes 2408456 | tf_op jit(solution)/shard_map/ppermute | solution.py:277
  106.3 19.3 %collective-permute-start.19 = (s16[392,256]{1,0:T(8,128)(2,1)S(1)}, s16[392,256]{1,0:T(8,128)(2,1)S(1)}, u32[]{:S(2)}, u32[]{:S(2)}) collective-permute-start(s16[392,256]{1,0:T(8,128)(2,1)S(1)} %stage2.11.refs_1_), channel_id=1, source_target_pairs={{0,16},{4,20},{8,24},{12,28},{16,0},{20,4},{24,8},{28,12},{1,17},{... | collective-permute-start | bytes 602120 | tf_op jit(solution)/shard_map/ppermute | solution.py:277
  113.3 35.9 %collective-permute-start.16 = (s16[392,512]{1,0:T(8,128)(2,1)}, s16[392,512]{1,0:T(8,128)(2,1)}, u32[]{:S(2)}, u32[]{:S(2)}) collective-permute-start(s16[392,512]{1,0:T(8,128)(2,1)} %stage1.14.refs_2_), channel_id=1, source_target_pairs={{0,8},{4,12},{8,0},{12,4},{16,24},{20,28},{24,16},{28,20},{1,9},{5... | collective-permute-start | bytes 1204232 | tf_op jit(solution)/shard_map/ppermute | solution.py:277
  116.2 15.5 %collective-permute-start.18 = (s16[392,256]{1,0:T(8,128)(2,1)S(1)}, s16[392,256]{1,0:T(8,128)(2,1)S(1)}, u32[]{:S(2)}, u32[]{:S(2)}) collective-permute-start(s16[392,256]{1,0:T(8,128)(2,1)S(1)} %stage2.12.refs_2_), channel_id=1, source_target_pairs={{0,16},{4,20},{8,24},{12,28},{16,0},{20,4},{24,8},{28,12},{1,17},{... | collective-permute-start | bytes 602120 | tf_op jit(solution)/shard_map/ppermute | solution.py:277
  120.4 37.0 %collective-permute-start.14 = (s16[392,256]{1,0:T(8,128)(2,1)}, s16[392,256]{1,0:T(8,128)(2,1)}, u32[]{:S(2)}, u32[]{:S(2)}) collective-permute-start(s16[392,256]{1,0:T(8,128)(2,1)} %stage2.13.refs_0_), channel_id=1, source_target_pairs={{0,16},{4,20},{8,24},{12,28},{16,0},{20,4},{24,8},{28,12},{1,17},{... | collective-permute-start | bytes 602120 | tf_op jit(solution)/shard_map/ppermute | solution.py:277
  125.6 28.3 %collective-permute-start.15 = (s16[392,512]{1,0:T(8,128)(2,1)}, s16[392,512]{1,0:T(8,128)(2,1)}, u32[]{:S(2)}, u32[]{:S(2)}) collective-permute-start(s16[392,512]{1,0:T(8,128)(2,1)} %stage0.16.refs_5_), channel_id=1, source_target_pairs={{0,4},{4,0},{8,12},{12,8},{16,20},{20,16},{24,28},{28,24},{1,5},{5... | collective-permute-start | bytes 1204232 | tf_op jit(solution)/shard_map/ppermute | solution.py:277
  135.3 28.3 %all-to-all-start.1 = ((s16[8,32,1152]{2,1,0:T(8,128)(2,1)}), s16[8,32,1152]{2,1,0:T(8,128)(2,1)}, u32[]{:S(2)}, u32[]{:S(2)}) async-start(s16[8,32,1152]{2,1,0:T(8,128)(2,1)} %bitcast.38), calls=%async_computation.1 | async-start | bytes 1179648 | tf_op jit(solution)/shard_map/all_to_all | solution.py:188
  142.2 18.5 %collective-permute-start.21 = (s16[392,512]{1,0:T(8,128)(2,1)S(1)}, s16[392,512]{1,0:T(8,128)(2,1)S(1)}, u32[]{:S(2)}, u32[]{:S(2)}) collective-permute-start(s16[392,512]{1,0:T(8,128)(2,1)S(1)} %stage0.17.refs_1_), channel_id=1, source_target_pairs={{0,4},{4,0},{8,12},{12,8},{16,20},{20,16},{24,28},{28,24},{1,5},{5... | collective-permute-start | bytes 1204232 | tf_op jit(solution)/shard_map/ppermute | solution.py:277
  147.7 18.7 %collective-permute-start.24 = (s16[392,512]{1,0:T(8,128)(2,1)}, s16[392,512]{1,0:T(8,128)(2,1)}, u32[]{:S(2)}, u32[]{:S(2)}) collective-permute-start(s16[392,512]{1,0:T(8,128)(2,1)} %stage1.15.refs_2_), channel_id=1, source_target_pairs={{0,8},{4,12},{8,0},{12,4},{16,24},{20,28},{24,16},{28,20},{1,9},{5... | collective-permute-start | bytes 1204232 | tf_op jit(solution)/shard_map/ppermute | solution.py:277
  151.5 26.9 %collective-permute-start.20 = (s16[392,256]{1,0:T(8,128)(2,1)S(1)}, s16[392,256]{1,0:T(8,128)(2,1)}, u32[]{:S(2)}, u32[]{:S(2)}) collective-permute-start(s16[392,256]{1,0:T(8,128)(2,1)S(1)} %stage2.14.refs_1_), channel_id=1, source_target_pairs={{0,16},{4,20},{8,24},{12,28},{16,0},{20,4},{24,8},{28,12},{1,17},{... | collective-permute-start | bytes 602120 | tf_op jit(solution)/shard_map/ppermute | solution.py:277
  156.9 15.2 %collective-permute-start.23 = (s16[392,256]{1,0:T(8,128)(2,1)}, s16[392,256]{1,0:T(8,128)(2,1)}, u32[]{:S(2)}, u32[]{:S(2)}) collective-permute-start(s16[392,256]{1,0:T(8,128)(2,1)} %stage1.16.refs_5_), channel_id=1, source_target_pairs={{0,16},{4,20},{8,24},{12,28},{16,0},{20,4},{24,8},{28,12},{1,17},{... | collective-permute-start | bytes 602120 | tf_op jit(solution)/shard_map/ppermute | solution.py:277
  (27 other events, 135.1 us)
